TPU v7x, 128 devices: a whole 4x4x4 slice. The times are simulated.
128 devices in a mesh: ctx: 16 (over x, y), head: 8 (over z, core).
Axes of the slice: x: 4, y: 4, z: 4, core: 2. Of those that a mesh axis runs over, the one named last changes fastest.
Arguments:
- tokens: bfloat16 [65536, 2048], P(('ctx', 'head')), may hold values from -6 to 6
- picks: int32 [16384], P(('ctx', 'head')), may hold values from 0 to 511, as said below
- counts: int32 [128], P(('ctx', 'head')), may hold values from 1 to 128, 8192 in all
- score: float32 [16384], P(('ctx', 'head')), may hold values from 0.25 to 1
- w_in: bfloat16 [2048, 8192], P(None, 'head'), may hold values from -0.125 to 0.125
- w_out: bfloat16 [8192, 2048], P('head'), may hold values from -0.0625 to 0.0625
- cotan: bfloat16 [16384, 2048], P(('ctx', 'head')), may hold values from -6 to 6
Outputs:
- heavy: bfloat16 [16384, 2048], P(('ctx', 'head'))
- grad_x: bfloat16 [65536, 2048], P(('ctx', 'head'))
- grad_score: float32 [16384], P(('ctx', 'head'))
- grad_in: float32 [2048, 8192], P('ctx', 'head')
- grad_out: float32 [8192, 2048], P('head', 'ctx')
Inputs may be any that keep to these rules, and one draw needn't show every extreme that they name: `picks`: the 128 entries of one device are distinct positions of that device's 512 tokens.
All inputs are finite; a program needn't handle non-finite values. No bound on the sum of `counts` on one device may be relied on, other than what follows from the above.
Results may differ from a plain program's by a relative error of at most 0.027.
Values may be sent and summed in bfloat16 or wider, within the bound.
No kernel may reach another device: no remote copies, remote signals or barrier semaphores. Data moves between devices by JAX's collectives and lax.ppermute only.
A program may use at most 128 MiB of HBM per device.

v0:
```python
import functools

import jax
import jax.numpy as jnp
from jax import lax
from jax.experimental import pallas as pl
from jax.experimental.pallas import tpu as pltpu
from jax.sharding import PartitionSpec as P

F32 = jnp.float32
BF16 = jnp.bfloat16
SIDE = 4
MIB = 1024 * 1024
LITTLE = pl.CostEstimate(flops=1, bytes_accessed=1, transcendentals=0)


def gelu_parts(u):
    c = 0.7978845608
    t = jnp.tanh(c * (u + 0.044715 * u * u * u))
    value = 0.5 * u * (1.0 + t)
    slope = 0.5 * (1.0 + t) + 0.5 * u * (1.0 - t * t) * c * (1.0 + 3.0 * 0.044715 * u * u)
    return (value, slope)


def move_x(v, by):
    perm = [(x * SIDE + y, ((x + by) % SIDE) * SIDE + y) for x in range(SIDE) for y in range(SIDE)]
    return lax.ppermute(v, "ctx", perm)


def move_y(v, by):
    perm = [(x * SIDE + y, x * SIDE + (y + by) % SIDE) for x in range(SIDE) for y in range(SIDE)]
    return lax.ppermute(v, "ctx", perm)


def move_lane(v, by):
    perm = [(z * 2 + c, ((z + (by if c == 0 else -by)) % SIDE) * 2 + c) for z in range(SIDE) for c in range(2)]
    return lax.ppermute(v, "head", perm)


def swap_core(v):
    return lax.ppermute(v, "head", [(i, i ^ 1) for i in range(2 * SIDE)])


def dot(a, b, dims):
    return lax.dot_general(a, b, ((dims[0], dims[1]), ((), ())), preferred_element_type=F32)


def params(mib):
    return pltpu.CompilerParams(vmem_limit_bytes=mib * MIB)


def whole(a):
    return pl.BlockSpec(a.shape, lambda *_: (0,) * a.ndim)


def take_rows(tokens, picks, counts, score, cotan):
    routed = picks.shape[0]
    n_tok, width = tokens.shape

    def body(counts_ref, tokens_ref, picks_ref, score_ref, cotan_ref, out_ref, me_ref):
        me_ref[0] = lax.axis_index("ctx").astype(jnp.int32)
        me_ref[1] = lax.axis_index("head").astype(jnp.int32)
        places = lax.broadcasted_iota(jnp.int32, (n_tok, routed), 0)
        slots = lax.broadcasted_iota(jnp.int32, (n_tok, routed), 1)
        hit = (places == picks_ref[...]) & (slots < counts_ref[0])
        one_hot = jnp.where(hit, 1.0, 0.0).astype(BF16)
        out_ref[0] = dot(one_hot, tokens_ref[...], ((0,), (0,))).astype(BF16)
        across = lax.broadcasted_iota(jnp.int32, (routed, routed), 0)
        along = lax.broadcasted_iota(jnp.int32, (routed, routed), 1)
        kept = (across == along) & (along < counts_ref[0])
        factor = jnp.sum(jnp.where(kept, score_ref[...], 0.0), axis=1, keepdims=True)
        out_ref[1] = (factor * cotan_ref[...].astype(F32)).astype(BF16)

    return pl.pallas_call(
        body,
        grid_spec=pltpu.PrefetchScalarGridSpec(
            num_scalar_prefetch=1,
            grid=(1,),
            in_specs=[
                whole(tokens),
                pl.BlockSpec((1, routed), lambda i, c: (0, 0)),
                pl.BlockSpec((1, routed), lambda i, c: (0, 0)),
                whole(cotan),
            ],
            out_specs=[
                pl.BlockSpec((2, routed, width), lambda i, c: (0, 0, 0)),
                pl.BlockSpec(memory_space=pltpu.SMEM),
            ],
        ),
        out_shape=[jax.ShapeDtypeStruct((2, routed, width), BF16), jax.ShapeDtypeStruct((2,), jnp.int32)],
        compiler_params=params(60),
        cost_estimate=LITTLE,
        name="take_rows",
    )(counts, tokens, picks[None, :], score[None, :], cotan)


IN_VMEM = pl.BlockSpec(memory_space=pltpu.VMEM)
IN_SMEM = pl.BlockSpec(memory_space=pltpu.SMEM)


def held(a):
    return pltpu.with_memory_space_constraint(a, pltpu.VMEM)


def on_held(body, arrays, shapes, name, me=None, spare=(), aliases={}):
    first = [] if me is None else [me]
    return pl.pallas_call(
        body,
        in_specs=[IN_SMEM] * len(first) + [IN_VMEM] * len(arrays) + [pl.BlockSpec(memory_space=pl.ANY)] * len(spare),
        out_specs=[IN_VMEM] * len(shapes),
        out_shape=[pltpu.VMEM(shape, dtype) for shape, dtype in shapes],
        input_output_aliases=aliases,
        compiler_params=params(12),
        cost_estimate=LITTLE,
        name=name,
    )(*first, *[held(a) for a in arrays], *[held(a) for a in spare])


def repeat(count, step, unrolled):
    if unrolled:
        for i in range(count):
            step(i)
    else:
        lax.fori_loop(0, count, lambda i, c: (step(i), c)[1], 0)


def span(i, size):
    at = i * size
    return pl.ds(at if isinstance(i, int) else pl.multiple_of(at, size), size)


def hidden_units(packs, w_in, w_out, unrolled=False):
    halves = [(i, h) for i, p in enumerate(packs) for h in range(len(p))]
    at = {p: k for k, p in enumerate(halves)}
    where_r = [at[(i, 0)] for i in range(len(packs))]
    where_d = [at[(i, len(p) - 1)] for i, p in enumerate(packs)]
    flat = [a for p in packs for a in p]
    n = len(packs)
    _, piece, width = flat[0].shape
    count = n * piece
    hid = w_in.shape[1]
    tile = hid // SIDE
    quarter = width // SIDE
    strip = quarter // SIDE

    def body(*refs):
        last = [refs[k].shape[0] - 1 for k in where_d]
        r = jnp.concatenate([refs[k][0] for k in where_r], axis=0)
        d = jnp.concatenate([refs[k][i] for k, i in zip(where_d, last)], axis=0)
        win_ref, wout_ref, hidden_ref, dpre_ref, turned_ref = refs[len(flat) :]

        def step(j):
            cols = span(j, tile)
            pre = dot(r, win_ref[:, cols], ((1,), (0,)))
            dhid = dot(d, wout_ref[cols, :], ((1,), (1,)))
            value, slope = gelu_parts(pre)
            hidden_ref[:, cols] = value.astype(BF16)
            dpre_ref[:, cols] = (dhid * slope).astype(BF16)
            for x in range(SIDE):
                to = span(j * SIDE + x, strip)
                for k in range(n):
                    turned_ref[pl.ds(k * piece, piece), to] = refs[where_d[k]][last[k], :, span(x * SIDE + j, strip)]

        repeat(SIDE, step, unrolled)

    shapes = [((count, hid), BF16), ((count, hid), BF16), ((count, width), BF16)]
    return on_held(body, flat + [w_in, w_out], shapes, "hidden_units")


def hold(w_in, w_out):
    def body(win_ref, wout_ref, win_out, wout_out, sems):
        copies = [
            pltpu.make_async_copy(win_ref, win_out, sems.at[0]),
            pltpu.make_async_copy(wout_ref, wout_out, sems.at[1]),
        ]
        for copy in copies:
            copy.start()
        for copy in copies:
            copy.wait()

    return pl.pallas_call(
        body,
        in_specs=[pl.BlockSpec(memory_space=pl.ANY)] * 2,
        out_specs=[pl.BlockSpec(memory_space=pltpu.VMEM)] * 2,
        out_shape=[pltpu.VMEM(w.shape, w.dtype) for w in (w_in, w_out)],
        scratch_shapes=[pltpu.SemaphoreType.DMA((2,))],
        compiler_params=params(4),
        cost_estimate=LITTLE,
        name="hold_weights",
    )(pltpu.with_memory_space_constraint(w_in, pltpu.HBM), pltpu.with_memory_space_constraint(w_out, pltpu.HBM))


def row_terms(hidden, dpre, w_in, w_out, piece, groups, first=0, held_terms=(), unrolled=False):
    count, hid = hidden.shape
    width = w_in.shape[0]
    n = count // (2 * piece)
    tile = width // SIDE

    def body(hidden_ref, dpre_ref, win_ref, wout_ref, *refs):
        outs = refs[len(held_terms) :]

        def step(j):
            cols = span(j, tile)
            ffn = dot(hidden_ref[...], wout_ref[:, cols], ((1,), (0,))).astype(BF16)
            dx = dot(dpre_ref[...], win_ref[cols, :], ((1,), (1,))).astype(BF16)
            for h in range(2):
                for k in range(n):
                    for s, v in enumerate((ffn, dx)):
                        outs[h][first + k, s, :, cols] = v[(h * n + k) * piece : (h * n + k + 1) * piece]

        repeat(SIDE, step, unrolled)

    shapes = [((groups, 2, piece, width), BF16)] * 2
    aliases = {4 + i: i for i in range(len(held_terms))}
    return on_held(body, [hidden, dpre, w_in, w_out], shapes, "row_terms", spare=held_terms, aliases=aliases)


FIRST_STEP = ((2, 0), (2, 1), (1, 1), (3, 0))
LATER_STEP = ((1, 0), (3, 1), (0, 0), (0, 1))


def make_blocks(steps, outs, make):
    if steps is FIRST_STEP:
        for i, (place, half) in enumerate(steps):
            outs[i % 2][i // 2] = make(place, half).astype(BF16)
    else:

        def step(i):
            place = jnp.where(i >= 2, 0, jnp.where(i == 0, 1, 3))
            half = jnp.where((i == 1) | (i == 3), 1, 0)
            outs[0][i] = make(place, half).astype(BF16)

        repeat(len(steps), step, False)


def block_shapes(steps, block):
    return [((2,) + block, BF16)] * 2 if steps is FIRST_STEP else [((len(steps),) + block, BF16)]


def in_blocks(me, packs, dpre, steps):
    n = len(packs)
    _, piece, width = packs[0].shape
    hid = dpre[0].shape[1]
    size = width // (2 * SIDE)
    each = n // len(dpre)

    def body(me_ref, *refs):
        def make(place, half):
            to = 2 * lax.rem(me_ref[0] // SIDE + place, SIDE) + half
            cols = pl.ds(pl.multiple_of(to * size, size), size)
            term = None
            for c in range(len(dpre)):
                r = jnp.concatenate([ref[0, :, cols] for ref in refs[c * each : (c + 1) * each]], axis=0)
                part = dot(r, refs[n + c][...], ((0,), (0,)))
                term = part if term is None else term + part
            return term

        make_blocks(steps, refs[n + len(dpre) :], make)

    return on_held(body, packs + dpre, block_shapes(steps, (size, hid)), "in_blocks", me)


def out_blocks(me, hidden, turned, steps):
    n = len(hidden)
    hid = hidden[0].shape[1]
    quarter = turned[0].shape[1] // SIDE

    def body(me_ref, *refs):
        def make(place, half):
            to = lax.rem(lax.rem(me_ref[0], SIDE) + place, SIDE)
            cols = pl.ds(pl.multiple_of(to * quarter, quarter), quarter)
            term = None
            for c in range(n):
                part = dot(refs[c][:, span(half, hid // 2)], refs[n + c][:, cols], ((0,), (0,)))
                term = part if term is None else term + part
            return term

        make_blocks(steps, refs[2 * n :], make)

    return on_held(body, hidden + turned, block_shapes(steps, (hid // 2, quarter)), "out_blocks", me)


def ring_total(me, later, below0, above0, below1, above1, rowwise):
    block = later.shape[1:]
    if rowwise:
        cut = (2 * block[0] // SIDE, block[1])
    else:
        cut = (2 * block[0], block[1] // SIDE)

    def body(me_ref, later_ref, b0, a0, b1, a1, keep_ref, next_ref, prev_ref, far_ref, sum_ref):
        half = block[0]
        rows = half // SIDE

        def step(j):
            cut_j = span(j, rows)
            first = later_ref[2, cut_j].astype(F32) + b0[cut_j].astype(F32) + a0[1, cut_j].astype(F32)
            second = later_ref[3, cut_j].astype(F32) + b1[1, cut_j].astype(F32) + a1[cut_j].astype(F32)
            sum_ref[cut_j, :] = first
            sum_ref[span(j + SIDE, rows), :] = second

        repeat(SIDE, step, False)
        if rowwise:
            at = lax.rem(me_ref[0], SIDE)
        else:
            at = me_ref[0] // SIDE
        for k, ref in ((0, keep_ref), (1, next_ref), (3, prev_ref), (2, far_ref)):
            to = lax.rem(at + k, SIDE)
            if rowwise:
                v = sum_ref[pl.ds(pl.multiple_of(to * cut[0], cut[0]), cut[0]), :]
            else:
                v = sum_ref[:, pl.ds(pl.multiple_of(to * cut[1], cut[1]), cut[1])]
            ref[...] = v.astype(ref.dtype)

    return pl.pallas_call(
        body,
        in_specs=[IN_SMEM] + [IN_VMEM] * 5,
        out_specs=[IN_VMEM] * 4,
        out_shape=[pltpu.VMEM(cut, F32)] + [pltpu.VMEM(cut, BF16)] * 3,
        scratch_shapes=[pltpu.VMEM((2 * block[0], block[1]), F32)],
        compiler_params=params(12),
        cost_estimate=LITTLE,
        name="ring_total",
    )(me, *[held(a) for a in (later, below0, above0, below1, above1)])


def add_up(*groups):
    flat = [a for g in groups for a in g]

    def body(*refs):
        at = 0
        for g, out_ref in zip(groups, refs[len(flat) :]):
            total = refs[at][...].astype(F32)
            for ref in refs[at + 1 : at + len(g)]:
                total += ref[...].astype(F32)
            out_ref[...] = total
            at += len(g)

    return pl.pallas_call(
        body,
        grid=(1,),
        in_specs=[whole(a) for a in flat],
        out_specs=[whole(g[0]) for g in groups],
        out_shape=[jax.ShapeDtypeStruct(g[0].shape, F32) for g in groups],
        compiler_params=params(10),
        cost_estimate=LITTLE,
        name="add_up",
    )(*flat)


def after(values, *deps):
    return lax.optimization_barrier((values, deps))[0]


def on_device(tokens, picks, counts, score, w_in, w_out, cotan):
    routed = picks.shape[0]
    n_tok = tokens.shape[0]

    own_mine, me = take_rows(tokens, picks, counts, score, cotan)
    w_in, w_out = hold(*after((w_in, w_out), own_mine))
    near_mine = move_lane(own_mine, 1)
    own_other = swap_core(own_mine)
    own = hidden_units([[own_mine], [own_other]], w_in, w_out)

    near_other = move_lane(own_other, 1)
    near_mine = after(near_mine, own)
    far_mine = move_lane(near_mine, 1)
    swapped_mine = [swap_core(near_mine[:1]), swap_core(near_mine[1:])]
    own_terms = row_terms(own[0], own[1], w_in, w_out, routed, 1)
    own_got = swap_core(own_terms[1])
    near_mine, swapped_mine = after((near_mine, swapped_mine), own_terms)
    near = hidden_units([[near_mine], swapped_mine], w_in, w_out)
    near_terms = row_terms(near[0], near[1], w_in, w_out, routed, 3)

    near_other = after(near_other, near)
    swapped_other = [swap_core(near_other[:1]), swap_core(near_other[1:])]
    swapped_other, own_got = after((swapped_other, own_got), near_terms)
    other = hidden_units([[near_other], swapped_other], w_in, w_out)
    near_terms = row_terms(other[0], other[1], w_in, w_out, routed, 3, 1, near_terms)

    far_mine = after(far_mine, other)
    far_packs = after([far_mine, swap_core(far_mine)], near_terms)
    far = hidden_units([[p] for p in far_packs], w_in, w_out, True)
    last_terms = row_terms(far[0], far[1], w_in, w_out, routed, 3, 2, near_terms, True)
    last_got = swap_core(last_terms[1])

    all_packs = [own_mine, own_other, near_mine, swapped_mine[0], near_other, swapped_other[0]] + far_packs
    hidden, dpre, turned = ([u[i] for u in (own, near, other, far)] for i in range(3))
    all_packs, dpre = after((all_packs, dpre), last_terms)
    in_up, in_down = in_blocks(me, all_packs, dpre, FIRST_STEP)
    in_below, in_above = move_x(in_up, 1), move_x(in_down, -1)

    hidden, turned = after((hidden, turned), in_up, in_down)
    out_up, out_down = out_blocks(me, hidden, turned, FIRST_STEP)
    out_below, out_above = move_y(out_up, 1), move_y(out_down, -1)

    last_got = after(last_got, out_up, out_down)
    to_far = (last_terms[0][2].astype(F32) + last_got[2].astype(F32)).astype(BF16)
    z_far = move_lane(to_far, -1)
    all_packs, dpre = after((all_packs, dpre), to_far)
    in_later = in_blocks(me, all_packs, dpre, LATER_STEP)[0]
    z_far = after(z_far, in_later)
    passed = jnp.pad(z_far.astype(F32)[None], ((0, 1), (0, 0), (0, 0), (0, 0)))
    to_near = (last_terms[0][:2].astype(F32) + last_got[:2].astype(F32) + passed).astype(BF16)
    z_near = move_lane(to_near, -1)
    hidden, turned = after((hidden, turned), to_near)
    out_later = out_blocks(me, hidden, turned, LATER_STEP)[0]

    def second_hop(later, from_below, from_above, move):
        up = (later[0].astype(F32) + from_below[0].astype(F32)).astype(BF16)
        down = (later[1].astype(F32) + from_above[0].astype(F32)).astype(BF16)
        return move(up, 1), move(down, -1), up, down

    in_below, in_above, out_below, out_above = after((in_below, in_above, out_below, out_above), out_later)
    in_hops = second_hop(in_later, in_below, in_above, move_x)
    out_hops = second_hop(out_later, out_below, out_above, move_y)
    in_total = ring_total(me, in_later, in_hops[0], in_above, in_below, in_hops[1], True)
    out_hops = after(out_hops[:2], in_total)
    z_near = after(z_near, in_total, out_hops)
    z_other = swap_core(z_near[1])

    def second_stage(total, move):
        keep, following, previous, far = total
        return keep, move(far, 2), move(following, 1), move(previous, -1)

    out_total = ring_total(me, out_later, out_hops[0], out_above, out_below, out_hops[1], False)
    in_total, out_total = after((in_total, out_total), z_other)
    in_parts = second_stage(in_total, move_y)
    out_parts = second_stage(out_total, move_x)

    back = (
        own_terms[0][0].astype(F32) + own_got[0].astype(F32) + z_near[0].astype(F32) + z_other.astype(F32)
    ).astype(BF16)
    ffn = back[0].astype(F32)
    heavy = (score[:, None] * ffn).astype(BF16)
    grad_score = jnp.sum(cotan.astype(F32) * ffn, axis=1)
    place = picks[:, None] == jnp.arange(n_tok, dtype=jnp.int32)[None, :]
    grad_x = dot(place.astype(BF16), back[1], ((0,), (0,))).astype(BF16)
    in_parts, out_parts = after((in_parts, out_parts), heavy, grad_x)
    grad_in, grad_out = add_up(in_parts, out_parts)
    return (heavy, grad_x, grad_score, grad_in, grad_out)


def solution(mesh):
    placed = (
        P(("ctx", "head"), None),
        P(("ctx", "head")),
        P(("ctx", "head")),
        P(("ctx", "head")),
        P(None, "head"),
        P("head", None),
        P(("ctx", "head"), None),
    )
    return jax.shard_map(
        on_device,
        mesh=mesh,
        in_specs=placed,
        out_specs=(
            P(("ctx", "head"), None),
            P(("ctx", "head"), None),
            P(("ctx", "head")),
            P("ctx", "head"),
            P("head", "ctx"),
        ),
        check_vma=False,
    )
```

profile of v0, /device:TPU:70, one launch (start us, length us, event | category | flops | bytes accessed | tf_op | source)
XLA Modules:
  0.0 130.9 jit_solution(13845113675215332429)
XLA Ops:
  1.3 3.2 %take_rows.1 = (bf16[2,128,2048]{2,1,0:T(8,128)(2,1)}, s32[2]{0:T(128)}) custom-call(s32[1]{0:T(128)S(6)} %copy.20.counts_ref, bf16[512,2048]{1,0:T(8,128)(2,1)} %tokens_ref.1, s32[1,128]{1,0:T(1,128)} %bitcast.31, f32[1,128]{1,0:T(1,128)} %bitcast.30, bf16[128,2048]{1,0:T(8,128)(2,1)} %cotan_ref.1), custom_call_target="tpu_custom_call" | custom-call | flops 1 | bytes 1 | tf_op jit(solution)/shard_map/take_rows/pallas_call | solution.py:74
  9.0 3.5 %hold_weights.1 = (bf16[2048,1024]{1,0:T(8,128)(2,1)S(1)}, bf16[1024,2048]{1,0:T(8,128)(2,1)S(1)}) custom-call(bf16[2048,1024]{1,0:T(8,128)(2,1)} %win_ref, bf16[1024,2048]{1,0:T(8,128)(2,1)} %wout_ref), custom_call_target="tpu_custom_call" | custom-call | flops 1 | bytes 1 | tf_op jit(solution)/shard_map/hold_weights/pallas_call | solution.py:181
  12.5 3.8 %hidden_units.4 = (bf16[256,1024]{1,0:T(8,128)(2,1)S(1)}, bf16[256,1024]{1,0:T(8,128)(2,1)S(1)}, bf16[256,2048]{1,0:T(8,128)(2,1)S(1)}) custom-call(bf16[2,128,2048]{2,1,0:T(8,128)(2,1)S(1)} %copy-done, bf16[2,128,2048]{2,1,0:T(8,128)(2,1)S(1)} %collective-permute-done.refs_1_, bf16[2048,1024]{1,0:T(8,128)(2,1)S(1)} %get-tuple-element.124.refs_2_.win_ref.refs_3_, ...), custom_call_target="tpu_custom_call" | custom-call | flops 1 | bytes 1 | tf_op jit(solution)/shard_map/hidden_units/pallas_call | solution.py:107
  16.3 3.3 %collective-permute-done.2.refs_0_.refs_2_ = bf16[2,128,2048]{2,1,0:T(8,128)(2,1)S(1)} collective-permute-done((bf16[2,128,2048]{2,1,0:T(8,128)(2,1)}, bf16[2,128,2048]{2,1,0:T(8,128)(2,1)S(1)}, u32[]{:S(2)}, u32[]{:S(2)}) %collective-permute-start.2) | collective-permute-done | bytes 1048608 | tf_op jit(solution)/shard_map/ppermute | solution.py:37
  20.3 2.8 %row_terms.4 = (bf16[1,2,128,2048]{3,2,1,0:T(8,128)(2,1)S(1)}, bf16[1,2,128,2048]{3,2,1,0:T(8,128)(2,1)S(1)}) custom-call(bf16[256,1024]{1,0:T(8,128)(2,1)S(1)} %get-tuple-element.196.hidden_ref.refs_0_, bf16[256,1024]{1,0:T(8,128)(2,1)S(1)} %get-tuple-element.191.dpre_ref.refs_8_, bf16[2048,1024]{1,0:T(8,128)(2,1)S(1)} %get-tuple-element.124.refs_2_.win_ref.refs_3_, ...), custom_call_target="tpu_custom_call" | custom-call | flops 1 | bytes 1 | tf_op jit(solution)/shard_map/row_terms/pallas_call | solution.py:107
  25.4 3.8 %hidden_units.5 = (bf16[256,1024]{1,0:T(8,128)(2,1)S(1)}, bf16[256,1024]{1,0:T(8,128)(2,1)S(1)}, bf16[256,2048]{1,0:T(8,128)(2,1)S(1)}) custom-call(bf16[2,128,2048]{2,1,0:T(8,128)(2,1)S(1)} %collective-permute-done.2.refs_0_.refs_2_, bf16[1,128,2048]{2,1,0:T(8,128)(2,1)S(1)} %collective-permute-done.3.refs_1_.refs_3_, ...), custom_call_target="tpu_custom_call" | custom-call | flops 1 | bytes 1 | tf_op jit(solution)/shard_map/hidden_units/pallas_call | solution.py:107
  31.6 2.8 %row_terms.5 = (bf16[3,2,128,2048]{3,2,1,0:T(8,128)(2,1)S(1)}, bf16[3,2,128,2048]{3,2,1,0:T(8,128)(2,1)S(1)}) custom-call(bf16[256,1024]{1,0:T(8,128)(2,1)S(1)} %get-tuple-element.197.hidden_ref.refs_1_, bf16[256,1024]{1,0:T(8,128)(2,1)S(1)} %get-tuple-element.192.dpre_ref.refs_9_, bf16[2048,1024]{1,0:T(8,128)(2,1)S(1)} %get-tuple-element.124.refs_2_.win_ref.refs_3_, ...), custom_call_target="tpu_custom_call" | custom-call | flops 1 | bytes 1 | tf_op jit(solution)/shard_map/row_terms/pallas_call | solution.py:107
  34.5 3.8 %hidden_units.6 = (bf16[256,1024]{1,0:T(8,128)(2,1)S(1)}, bf16[256,1024]{1,0:T(8,128)(2,1)S(1)}, bf16[256,2048]{1,0:T(8,128)(2,1)S(1)}) custom-call(bf16[2,128,2048]{2,1,0:T(8,128)(2,1)S(1)} %collective-permute-done.1.refs_0_.refs_4_, bf16[1,128,2048]{2,1,0:T(8,128)(2,1)S(1)} %collective-permute-done.5.refs_1_.refs_5_, ...), custom_call_target="tpu_custom_call" | custom-call | flops 1 | bytes 1 | tf_op jit(solution)/shard_map/hidden_units/pallas_call | solution.py:107
  38.3 3.9 %collective-permute-done.8.refs_0_.refs_6_ = bf16[2,128,2048]{2,1,0:T(8,128)(2,1)S(1)} collective-permute-done((bf16[2,128,2048]{2,1,0:T(8,128)(2,1)S(1)}, bf16[2,128,2048]{2,1,0:T(8,128)(2,1)S(1)}, u32[]{:S(2)}, u32[]{:S(2)}) %collective-permute-start.8) | collective-permute-done | bytes 1048608 | tf_op jit(solution)/shard_map/ppermute | solution.py:37
  42.1 2.8 %row_terms.6 = (bf16[3,2,128,2048]{3,2,1,0:T(8,128)(2,1)S(1)}, bf16[3,2,128,2048]{3,2,1,0:T(8,128)(2,1)S(1)}) custom-call(bf16[256,1024]{1,0:T(8,128)(2,1)S(1)} %get-tuple-element.198.hidden_ref.refs_2_, bf16[256,1024]{1,0:T(8,128)(2,1)S(1)} %get-tuple-element.193.dpre_ref.refs_10_, ...), custom_call_target="tpu_custom_call", output_to_operand_aliasing={{0}: (4, {}), {1}: (5, {})} | custom-call | flops 1 | bytes 1 | tf_op jit(solution)/shard_map/row_terms/pallas_call | solution.py:107
  45.0 2.9 %hidden_units.7 = (bf16[256,1024]{1,0:T(8,128)(2,1)S(1)}, bf16[256,1024]{1,0:T(8,128)(2,1)S(1)}, bf16[256,2048]{1,0:T(8,128)(2,1)S(1)}) custom-call(bf16[2,128,2048]{2,1,0:T(8,128)(2,1)S(1)} %collective-permute-done.8.refs_0_.refs_6_, bf16[2,128,2048]{2,1,0:T(8,128)(2,1)S(1)} %collective-permute-done.9.refs_1_.refs_7_, ...), custom_call_target="tpu_custom_call" | custom-call | flops 1 | bytes 1 | tf_op jit(solution)/shard_map/hidden_units/pallas_call | solution.py:107
  47.9 2.4 %row_terms.7 = (bf16[3,2,128,2048]{3,2,1,0:T(8,128)(2,1)S(1)}, bf16[3,2,128,2048]{3,2,1,0:T(8,128)(2,1)S(1)}) custom-call(bf16[256,1024]{1,0:T(8,128)(2,1)S(1)} %get-tuple-element.199.hidden_ref.refs_3_, bf16[256,1024]{1,0:T(8,128)(2,1)S(1)} %get-tuple-element.194.dpre_ref.refs_11_, ...), custom_call_target="tpu_custom_call", output_to_operand_aliasing={{0}: (4, {}), {1}: (5, {})} | custom-call | flops 1 | bytes 1 | tf_op jit(solution)/shard_map/row_terms/pallas_call | solution.py:107
  50.9 2.9 %in_blocks.2 = (bf16[2,256,1024]{2,1,0:T(8,128)(2,1)S(1)}, bf16[2,256,1024]{2,1,0:T(8,128)(2,1)S(1)}) custom-call(s32[2]{0:T(128)S(1)} %copy-done.1, bf16[2,128,2048]{2,1,0:T(8,128)(2,1)S(1)} %copy-done, bf16[2,128,2048]{2,1,0:T(8,128)(2,1)S(1)} %collective-permute-done.refs_1_, bf16[2,128,2048]{2,1,0:T(8,128)(2,1)S(1)} %collective-permute-done.2.refs_0_.refs_2_, ...), custom_call_target="tpu_custom_call" | custom-call | flops 1 | bytes 1 | tf_op jit(solution)/shard_map/in_blocks/pallas_call | solution.py:107
  53.8 2.9 %out_blocks.2 = (bf16[2,512,512]{2,1,0:T(8,128)(2,1)S(1)}, bf16[2,512,512]{2,1,0:T(8,128)(2,1)S(1)}) custom-call(s32[2]{0:T(128)S(1)} %copy-done.1, bf16[256,1024]{1,0:T(8,128)(2,1)S(1)} %get-tuple-element.196.hidden_ref.refs_0_, bf16[256,1024]{1,0:T(8,128)(2,1)S(1)} %get-tuple-element.197.hidden_ref.refs_1_, ...), custom_call_target="tpu_custom_call" | custom-call | flops 1 | bytes 1 | tf_op jit(solution)/shard_map/out_blocks/pallas_call | solution.py:107
  62.6 3.6 %in_blocks.3.later_ref = bf16[4,256,1024]{2,1,0:T(8,128)(2,1)S(1)} custom-call(s32[2]{0:T(128)S(1)} %copy-done.1, bf16[2,128,2048]{2,1,0:T(8,128)(2,1)S(1)} %copy-done, bf16[2,128,2048]{2,1,0:T(8,128)(2,1)S(1)} %collective-permute-done.refs_1_, bf16[2,128,2048]{2,1,0:T(8,128)(2,1)S(1)} %collective-permute-done.2.refs_0_.refs_2_, ...), custom_call_target="tpu_custom_call" | custom-call | flops 1 | bytes 1 | tf_op jit(solution)/shard_map/in_blocks/pallas_call | solution.py:107
  66.2 5.8 %collective-permute-done.11 = bf16[2,128,2048]{2,1,0:T(8,128)(2,1)S(1)} collective-permute-done((bf16[2,128,2048]{2,1,0:T(8,128)(2,1)S(1)}, bf16[2,128,2048]{2,1,0:T(8,128)(2,1)S(1)}, u32[]{:S(2)}, u32[]{:S(2)}) %collective-permute-start.11) | collective-permute-done | bytes 1048608 | tf_op jit(solution)/shard_map/ppermute | solution.py:37
  73.2 3.5 %out_blocks.3.later_ref = bf16[4,512,512]{2,1,0:T(8,128)(2,1)S(1)} custom-call(s32[2]{0:T(128)S(1)} %copy-done.1, bf16[256,1024]{1,0:T(8,128)(2,1)S(1)} %get-tuple-element.196.hidden_ref.refs_0_, bf16[256,1024]{1,0:T(8,128)(2,1)S(1)} %get-tuple-element.197.hidden_ref.refs_1_, bf16[256,1024]{1,0:T(8,128)(2,1)S(1)} %get-tuple-element.198.hidden_ref.refs_2_, ...), custom_call_target="tpu_custom_call" | custom-call | flops 1 | bytes 1 | tf_op jit(solution)/shard_map/out_blocks/pallas_call | solution.py:107
  76.7 5.9 %collective-permute-done.13.b1 = bf16[2,256,1024]{2,1,0:T(8,128)(2,1)S(1)} collective-permute-done((bf16[2,256,1024]{2,1,0:T(8,128)(2,1)S(1)}, bf16[2,256,1024]{2,1,0:T(8,128)(2,1)S(1)}, u32[]{:S(2)}, u32[]{:S(2)}) %collective-permute-start.13) | collective-permute-done | bytes 1048608 | tf_op jit(solution)/shard_map/ppermute | solution.py:27
  88.1 2.4 %collective-permute-start.17 = (bf16[256,1024]{1,0:T(8,128)(2,1)S(1)}, bf16[256,1024]{1,0:T(8,128)(2,1)S(1)}, u32[]{:S(2)}, u32[]{:S(2)}) collective-permute-start(bf16[256,1024]{1,0:T(8,128)(2,1)S(1)} %get-tuple-element.240), channel_id=1, source_target_pairs={{0,32},{8,40},{16,48},{24,56},{32,64},{40,72},{48,80},{56,88},{64,... | collective-permute-start | bytes 1572872 | tf_op jit(solution)/shard_map/ppermute | solution.py:27
  90.8 3.0 %collective-permute-start.20 = (bf16[512,512]{1,0:T(8,128)(2,1)S(1)}, bf16[512,512]{1,0:T(8,128)(2,1)S(1)}, u32[]{:S(2)}, u32[]{:S(2)}) collective-permute-start(bf16[512,512]{1,0:T(8,128)(2,1)S(1)} %get-tuple-element.237), channel_id=1, source_target_pairs={{0,24},{8,0},{16,8},{24,16},{32,56},{40,32},{48,40},{56,48},{64,88... | collective-permute-start | bytes 1572872 | tf_op jit(solution)/shard_map/ppermute | solution.py:32
  93.9 8.5 %collective-permute-done.18.a1 = bf16[256,1024]{1,0:T(8,128)(2,1)S(1)} collective-permute-done((bf16[256,1024]{1,0:T(8,128)(2,1)S(1)}, bf16[256,1024]{1,0:T(8,128)(2,1)S(1)}, u32[]{:S(2)}, u32[]{:S(2)}) %collective-permute-start.18) | collective-permute-done | bytes 524320 | tf_op jit(solution)/shard_map/ppermute | solution.py:27
  104.7 3.4 %collective-permute-done.19.b0 = bf16[512,512]{1,0:T(8,128)(2,1)S(1)} collective-permute-done((bf16[512,512]{1,0:T(8,128)(2,1)S(1)}, bf16[512,512]{1,0:T(8,128)(2,1)S(1)}, u32[]{:S(2)}, u32[]{:S(2)}) %collective-permute-start.19) | collective-permute-done | bytes 524320 | tf_op jit(solution)/shard_map/ppermute | solution.py:32
  123.2 2.9 %collective-permute-done.23.refs_2_ = bf16[128,1024]{1,0:T(8,128)(2,1)S(1)} collective-permute-done((bf16[128,1024]{1,0:T(8,128)(2,1)S(1)}, bf16[128,1024]{1,0:T(8,128)(2,1)S(1)}, u32[]{:S(2)}, u32[]{:S(2)}) %collective-permute-start.23) | collective-permute-done | bytes 262176 | tf_op jit(solution)/shard_map/ppermute | solution.py:32
  127.4 2.4 %collective-permute-done.27.refs_7_ = bf16[1024,128]{1,0:T(8,128)(2,1)S(1)} collective-permute-done((bf16[1024,128]{1,0:T(8,128)(2,1)S(1)}, bf16[1024,128]{1,0:T(8,128)(2,1)S(1)}, u32[]{:S(2)}, u32[]{:S(2)}) %collective-permute-start.27) | collective-permute-done | bytes 262176 | tf_op jit(solution)/shard_map/ppermute | solution.py:27
  (69 shorter events, 42.9 us)
Async XLA Ops:
  4.6 15.1 %collective-permute-start.2 = (bf16[2,128,2048]{2,1,0:T(8,128)(2,1)}, bf16[2,128,2048]{2,1,0:T(8,128)(2,1)S(1)}, u32[]{:S(2)}, u32[]{:S(2)}) collective-permute-start(bf16[2,128,2048]{2,1,0:T(8,128)(2,1)} %get-tuple-element.183.refs_0_), channel_id=1, source_target_pairs={{0,2},{1,7},{2,4},{3,1},{4,6},{5,3},{6,0},{7,5},{8,10},{9,15},{10,... | collective-permute-start | bytes 3145736 | tf_op jit(solution)/shard_map/ppermute | solution.py:37
  7.4 23.5 %collective-permute-start.1 = (bf16[2,128,2048]{2,1,0:T(8,128)(2,1)S(1)}, bf16[2,128,2048]{2,1,0:T(8,128)(2,1)S(1)}, u32[]{:S(2)}, u32[]{:S(2)}) collective-permute-start(bf16[2,128,2048]{2,1,0:T(8,128)(2,1)S(1)} %collective-permute-done.refs_1_), channel_id=1, source_target_pairs={{0,2},{1,7},{2,4},{3,1},{4,6},{5,3},{6,0},{7,5},{8,10},{9,15},{10,... | collective-permute-start | bytes 3145736 | tf_op jit(solution)/shard_map/ppermute | solution.py:37
  19.8 5.6 %collective-permute-start.4 = (bf16[1,128,2048]{2,1,0:T(8,128)(2,1)S(1)}, bf16[1,128,2048]{2,1,0:T(8,128)(2,1)S(1)}, u32[]{:S(2)}, u32[]{:S(2)}) collective-permute-start(bf16[1,128,2048]{2,1,0:T(8,128)(2,1)S(1)} %get-tuple-element.245), channel_id=1, source_target_pairs={{0,1},{1,0},{2,3},{3,2},{4,5},{5,4},{6,7},{7,6},{8,9},{9,8},{10,11... | collective-permute-start | bytes 1572872 | tf_op jit(solution)/shard_map/ppermute | solution.py:41
  19.8 5.5 %collective-permute-start.3 = (bf16[1,128,2048]{2,1,0:T(8,128)(2,1)S(1)}, bf16[1,128,2048]{2,1,0:T(8,128)(2,1)S(1)}, u32[]{:S(2)}, u32[]{:S(2)}) collective-permute-start(bf16[1,128,2048]{2,1,0:T(8,128)(2,1)S(1)} %get-tuple-element.246), channel_id=1, source_target_pairs={{0,1},{1,0},{2,3},{3,2},{4,5},{5,4},{6,7},{7,6},{8,9},{9,8},{10,11... | collective-permute-start | bytes 1572872 | tf_op jit(solution)/shard_map/ppermute | solution.py:41
  23.2 11.2 %collective-permute-start.7 = (bf16[1,2,128,2048]{3,2,1,0:T(8,128)(2,1)S(1)}, bf16[1,2,128,2048]{3,2,1,0:T(8,128)(2,1)S(1)}, u32[]{:S(2)}, u32[]{:S(2)}) collective-permute-start(bf16[1,2,128,2048]{3,2,1,0:T(8,128)(2,1)S(1)} %get-tuple-element.131), channel_id=1, source_target_pairs={{0,1},{1,0},{2,3},{3,2},{4,5},{5,4},{6,7},{7,6},{8,9},{9,8},{10,11... | collective-permute-start | bytes 3145736 | tf_op jit(solution)/shard_map/ppermute | solution.py:41
  23.4 18.7 %collective-permute-start.8 = (bf16[2,128,2048]{2,1,0:T(8,128)(2,1)S(1)}, bf16[2,128,2048]{2,1,0:T(8,128)(2,1)S(1)}, u32[]{:S(2)}, u32[]{:S(2)}) collective-permute-start(bf16[2,128,2048]{2,1,0:T(8,128)(2,1)S(1)} %collective-permute-done.2.refs_0_.refs_2_), channel_id=1, source_target_pairs={{0,2},{1,7},{2,4},{3,1},{4,6},{5,3},{6,0},{7,5},{8,10},{9,15},{10,... | collective-permute-start | bytes 3145736 | tf_op jit(solution)/shard_map/ppermute | solution.py:37
  31.0 3.5 %collective-permute-start.6 = (bf16[1,128,2048]{2,1,0:T(8,128)(2,1)S(1)}, bf16[1,128,2048]{2,1,0:T(8,128)(2,1)S(1)}, u32[]{:S(2)}, u32[]{:S(2)}) collective-permute-start(bf16[1,128,2048]{2,1,0:T(8,128)(2,1)S(1)} %get-tuple-element.243), channel_id=1, source_target_pairs={{0,1},{1,0},{2,3},{3,2},{4,5},{5,4},{6,7},{7,6},{8,9},{9,8},{10,11... | collective-permute-start | bytes 1572872 | tf_op jit(solution)/shard_map/ppermute | solution.py:41
  50.3 6.5 %collective-permute-start.10 = (bf16[3,2,128,2048]{3,2,1,0:T(8,128)(2,1)S(1)}, bf16[3,2,128,2048]{3,2,1,0:T(8,128)(2,1)S(1)}, u32[]{:S(2)}, u32[]{:S(2)}) collective-permute-start(bf16[3,2,128,2048]{3,2,1,0:T(8,128)(2,1)S(1)} %get-tuple-element.155), channel_id=1, source_target_pairs={{0,1},{1,0},{2,3},{3,2},{4,5},{5,4},{6,7},{7,6},{8,9},{9,8},{10,11... | collective-permute-start | bytes 9437192 | tf_op jit(solution)/shard_map/ppermute | solution.py:41
  57.1 14.9 %collective-permute-start.11 = (bf16[2,128,2048]{2,1,0:T(8,128)(2,1)S(1)}, bf16[2,128,2048]{2,1,0:T(8,128)(2,1)S(1)}, u32[]{:S(2)}, u32[]{:S(2)}) collective-permute-start(bf16[2,128,2048]{2,1,0:T(8,128)(2,1)S(1)} %fusion.3), channel_id=1, source_target_pairs={{0,6},{1,3},{2,0},{3,5},{4,2},{5,7},{6,4},{7,1},{8,14},{9,11},{10,... | collective-permute-start | bytes 3145736 | tf_op jit(solution)/shard_map/ppermute | solution.py:37
  57.3 25.3 %collective-permute-start.13 = (bf16[2,256,1024]{2,1,0:T(8,128)(2,1)S(1)}, bf16[2,256,1024]{2,1,0:T(8,128)(2,1)S(1)}, u32[]{:S(2)}, u32[]{:S(2)}) collective-permute-start(bf16[2,256,1024]{2,1,0:T(8,128)(2,1)S(1)} %get-tuple-element.170), channel_id=1, source_target_pairs={{0,32},{8,40},{16,48},{24,56},{32,64},{40,72},{48,80},{56,88},{64,... | collective-permute-start | bytes 3145736 | tf_op jit(solution)/shard_map/ppermute | solution.py:27
  57.8 26.8 %collective-permute-start.14 = (bf16[2,256,1024]{2,1,0:T(8,128)(2,1)S(1)}, bf16[2,256,1024]{2,1,0:T(8,128)(2,1)S(1)}, u32[]{:S(2)}, u32[]{:S(2)}) collective-permute-start(bf16[2,256,1024]{2,1,0:T(8,128)(2,1)S(1)} %get-tuple-element.171), channel_id=1, source_target_pairs={{0,96},{8,104},{16,112},{24,120},{32,0},{40,8},{48,16},{56,24},{64... | collective-permute-start | bytes 3145736 | tf_op jit(solution)/shard_map/ppermute | solution.py:27
  59.3 27.0 %collective-permute-start.15 = (bf16[2,512,512]{2,1,0:T(8,128)(2,1)S(1)}, bf16[2,512,512]{2,1,0:T(8,128)(2,1)S(1)}, u32[]{:S(2)}, u32[]{:S(2)}) collective-permute-start(bf16[2,512,512]{2,1,0:T(8,128)(2,1)S(1)} %get-tuple-element.180), channel_id=1, source_target_pairs={{0,8},{8,16},{16,24},{24,0},{32,40},{40,48},{48,56},{56,32},{64,72... | collective-permute-start | bytes 3145736 | tf_op jit(solution)/shard_map/ppermute | solution.py:32
  60.9 26.0 %collective-permute-start.16 = (bf16[2,512,512]{2,1,0:T(8,128)(2,1)S(1)}, bf16[2,512,512]{2,1,0:T(8,128)(2,1)S(1)}, u32[]{:S(2)}, u32[]{:S(2)}) collective-permute-start(bf16[2,512,512]{2,1,0:T(8,128)(2,1)S(1)} %get-tuple-element.181), channel_id=1, source_target_pairs={{0,24},{8,0},{16,8},{24,16},{32,56},{40,32},{48,40},{56,48},{64,88... | collective-permute-start | bytes 3145736 | tf_op jit(solution)/shard_map/ppermute | solution.py:32
  73.0 35.1 %collective-permute-start.12 = (bf16[2,2,128,2048]{3,2,1,0:T(8,128)(2,1)S(1)}, bf16[2,2,128,2048]{3,2,1,0:T(8,128)(2,1)S(1)}, u32[]{:S(2)}, u32[]{:S(2)}) collective-permute-start(bf16[2,2,128,2048]{3,2,1,0:T(8,128)(2,1)S(1)} %add_convert_fusion), channel_id=1, source_target_pairs={{0,6},{1,3},{2,0},{3,5},{4,2},{5,7},{6,4},{7,1},{8,14},{9,11},{10,... | collective-permute-start | bytes 6291464 | tf_op jit(solution)/shard_map/ppermute | solution.py:37
  87.2 15.1 %collective-permute-start.18 = (bf16[256,1024]{1,0:T(8,128)(2,1)S(1)}, bf16[256,1024]{1,0:T(8,128)(2,1)S(1)}, u32[]{:S(2)}, u32[]{:S(2)}) collective-permute-start(bf16[256,1024]{1,0:T(8,128)(2,1)S(1)} %get-tuple-element.239), channel_id=1, source_target_pairs={{0,96},{8,104},{16,112},{24,120},{32,0},{40,8},{48,16},{56,24},{64... | collective-permute-start | bytes 1572872 | tf_op jit(solution)/shard_map/ppermute | solution.py:27
  88.1 14.2 %collective-permute-start.17 = (bf16[256,1024]{1,0:T(8,128)(2,1)S(1)}, bf16[256,1024]{1,0:T(8,128)(2,1)S(1)}, u32[]{:S(2)}, u32[]{:S(2)}) collective-permute-start(bf16[256,1024]{1,0:T(8,128)(2,1)S(1)} %get-tuple-element.240), channel_id=1, source_target_pairs={{0,32},{8,40},{16,48},{24,56},{32,64},{40,72},{48,80},{56,88},{64,... | collective-permute-start | bytes 1572872 | tf_op jit(solution)/shard_map/ppermute | solution.py:27
  90.8 13.9 %collective-permute-start.20 = (bf16[512,512]{1,0:T(8,128)(2,1)S(1)}, bf16[512,512]{1,0:T(8,128)(2,1)S(1)}, u32[]{:S(2)}, u32[]{:S(2)}) collective-permute-start(bf16[512,512]{1,0:T(8,128)(2,1)S(1)} %get-tuple-element.237), channel_id=1, source_target_pairs={{0,24},{8,0},{16,8},{24,16},{32,56},{40,32},{48,40},{56,48},{64,88... | collective-permute-start | bytes 1572872 | tf_op jit(solution)/shard_map/ppermute | solution.py:32
  93.9 14.3 %collective-permute-start.19 = (bf16[512,512]{1,0:T(8,128)(2,1)S(1)}, bf16[512,512]{1,0:T(8,128)(2,1)S(1)}, u32[]{:S(2)}, u32[]{:S(2)}) collective-permute-start(bf16[512,512]{1,0:T(8,128)(2,1)S(1)} %get-tuple-element.238), channel_id=1, source_target_pairs={{0,8},{8,16},{16,24},{24,0},{32,40},{40,48},{48,56},{56,32},{64,72... | collective-permute-start | bytes 1572872 | tf_op jit(solution)/shard_map/ppermute | solution.py:32
  111.0 10.7 %collective-permute-start.22 = (bf16[128,1024]{1,0:T(8,128)(2,1)S(1)}, bf16[128,1024]{1,0:T(8,128)(2,1)S(1)}, u32[]{:S(2)}, u32[]{:S(2)}) collective-permute-start(bf16[128,1024]{1,0:T(8,128)(2,1)S(1)} %get-tuple-element.220), channel_id=1, source_target_pairs={{0,16},{8,24},{16,0},{24,8},{32,48},{40,56},{48,32},{56,40},{64,80... | collective-permute-start | bytes 786440 | tf_op jit(solution)/shard_map/ppermute | solution.py:32
  111.0 15.2 %collective-permute-start.23 = (bf16[128,1024]{1,0:T(8,128)(2,1)S(1)}, bf16[128,1024]{1,0:T(8,128)(2,1)S(1)}, u32[]{:S(2)}, u32[]{:S(2)}) collective-permute-start(bf16[128,1024]{1,0:T(8,128)(2,1)S(1)} %get-tuple-element.221), channel_id=1, source_target_pairs={{0,8},{8,16},{16,24},{24,0},{32,40},{40,48},{48,56},{56,32},{64,72... | collective-permute-start | bytes 786440 | tf_op jit(solution)/shard_map/ppermute | solution.py:32
  112.1 14.0 %collective-permute-start.24 = (bf16[128,1024]{1,0:T(8,128)(2,1)S(1)}, bf16[128,1024]{1,0:T(8,128)(2,1)S(1)}, u32[]{:S(2)}, u32[]{:S(2)}) collective-permute-start(bf16[128,1024]{1,0:T(8,128)(2,1)S(1)} %get-tuple-element.222), channel_id=1, source_target_pairs={{0,24},{8,0},{16,8},{24,16},{32,56},{40,32},{48,40},{56,48},{64,88... | collective-permute-start | bytes 786440 | tf_op jit(solution)/shard_map/ppermute | solution.py:32
  114.2 11.9 %collective-permute-start.25 = (bf16[1024,128]{1,0:T(8,128)(2,1)S(1)}, bf16[1024,128]{1,0:T(8,128)(2,1)S(1)}, u32[]{:S(2)}, u32[]{:S(2)}) collective-permute-start(bf16[1024,128]{1,0:T(8,128)(2,1)S(1)} %get-tuple-element.224), channel_id=1, source_target_pairs={{0,64},{8,72},{16,80},{24,88},{32,96},{40,104},{48,112},{56,120},{... | collective-permute-start | bytes 786440 | tf_op jit(solution)/shard_map/ppermute | solution.py:27
  114.4 13.0 %collective-permute-start.26 = (bf16[1024,128]{1,0:T(8,128)(2,1)S(1)}, bf16[1024,128]{1,0:T(8,128)(2,1)S(1)}, u32[]{:S(2)}, u32[]{:S(2)}) collective-permute-start(bf16[1024,128]{1,0:T(8,128)(2,1)S(1)} %get-tuple-element.225), channel_id=1, source_target_pairs={{0,32},{8,40},{16,48},{24,56},{32,64},{40,72},{48,80},{56,88},{64,... | collective-permute-start | bytes 786440 | tf_op jit(solution)/shard_map/ppermute | solution.py:27
  121.7 8.1 %collective-permute-start.27 = (bf16[1024,128]{1,0:T(8,128)(2,1)S(1)}, bf16[1024,128]{1,0:T(8,128)(2,1)S(1)}, u32[]{:S(2)}, u32[]{:S(2)}) collective-permute-start(bf16[1024,128]{1,0:T(8,128)(2,1)S(1)} %get-tuple-element.226), channel_id=1, source_target_pairs={{0,96},{8,104},{16,112},{24,120},{32,0},{40,8},{48,16},{56,24},{64... | collective-permute-start | bytes 786440 | tf_op jit(solution)/shard_map/ppermute | solution.py:27
  (9 other events, 38.2 us)
where the time goes:
time: 131 us
  waiting for transfers between devices  49.6 us (38%)
  Pallas kernels  48.1 us (37%)
  starting transfers between devices  24.9 us (19%)
  other arithmetic  4.29 us (3%)
  matrix products  2.14 us (2%)
  between operations  1.6 us (1%)
    pallas_call x12, Pallas kernels, on_held(): pl.pallas_call(body, in_specs=[IN_SMEM] * len(first) + [IN_VMEM] * len(ar...  38.1 us
    ppermute x7, waiting for transfers between devices, move_x(): return lax.ppermute(v, 'ctx', perm)  20 us
    ppermute x5, waiting for transfers between devices, move_lane(): return lax.ppermute(v, 'head', perm)  14.7 us
    ppermute x7, waiting for transfers between devices, move_y(): return lax.ppermute(v, 'ctx', perm)  12.2 us
    ppermute x7, starting transfers between devices, move_y(): return lax.ppermute(v, 'ctx', perm)  9.5 us
    ppermute x7, starting transfers between devices, move_x(): return lax.ppermute(v, 'ctx', perm)  7.6 us
    ppermute x5, starting transfers between devices, move_lane(): return lax.ppermute(v, 'head', perm)  5.66 us
    pallas_call x1, Pallas kernels, hold(): pl.pallas_call(body, in_specs=[pl.BlockSpec(memory_space=pl.ANY)] * 2, ou...  3.48 us
  transfers between devices with their start and end apart: 28, of which 17 were waited for; matrix products, arithmetic and copies ran while one was open for 5% of the time, Pallas kernels for 29%

commit v1 on v0

--- a/solution.py
+++ b/solution.py
@@ -12,6 +12,8 @@
 SIDE = 4
 MIB = 1024 * 1024
 LITTLE = pl.CostEstimate(flops=1, bytes_accessed=1, transcendentals=0)
+IN_VMEM = pl.BlockSpec(memory_space=pltpu.VMEM)
+IN_SMEM = pl.BlockSpec(memory_space=pltpu.SMEM)
 
 
 def gelu_parts(u):
@@ -56,46 +58,61 @@
 def take_rows(tokens, picks, counts, score, cotan):
     routed = picks.shape[0]
     n_tok, width = tokens.shape
-
-    def body(counts_ref, tokens_ref, picks_ref, score_ref, cotan_ref, out_ref, me_ref):
+    parts = 2
+    part = width // parts
+
+    def body(counts_ref, picks_hbm, score_hbm, tokens_ref, cotan_ref, out_ref, me_ref, *scratch):
+        rows_in, cotan_in, picks_ref, score_ref, sems = scratch
+        small = [
+            pltpu.make_async_copy(picks_hbm, picks_ref, sems.at[parts + 1]),
+            pltpu.make_async_copy(score_hbm, score_ref, sems.at[parts + 2]),
+        ]
+        for copy in small:
+            copy.start()
+        copies = [pltpu.make_async_copy(cotan_ref, cotan_in, sems.at[parts])]
+        for p in range(parts):
+            cols = pl.ds(p * part, part)
+            copies.append(pltpu.make_async_copy(tokens_ref.at[:, cols], rows_in.at[p], sems.at[p]))
+        for copy in copies:
+            copy.start()
         me_ref[0] = lax.axis_index("ctx").astype(jnp.int32)
         me_ref[1] = lax.axis_index("head").astype(jnp.int32)
+        for copy in small:
+            copy.wait()
         places = lax.broadcasted_iota(jnp.int32, (n_tok, routed), 0)
         slots = lax.broadcasted_iota(jnp.int32, (n_tok, routed), 1)
         hit = (places == picks_ref[...]) & (slots < counts_ref[0])
         one_hot = jnp.where(hit, 1.0, 0.0).astype(BF16)
-        out_ref[0] = dot(one_hot, tokens_ref[...], ((0,), (0,))).astype(BF16)
         across = lax.broadcasted_iota(jnp.int32, (routed, routed), 0)
         along = lax.broadcasted_iota(jnp.int32, (routed, routed), 1)
         kept = (across == along) & (along < counts_ref[0])
         factor = jnp.sum(jnp.where(kept, score_ref[...], 0.0), axis=1, keepdims=True)
-        out_ref[1] = (factor * cotan_ref[...].astype(F32)).astype(BF16)
-
+        copies[0].wait()
+        out_ref[1] = (factor * cotan_in[...].astype(F32)).astype(BF16)
+        for p in range(parts):
+            copies[1 + p].wait()
+            out_ref[0, :, pl.ds(p * part, part)] = dot(one_hot, rows_in[p], ((0,), (0,))).astype(BF16)
+
+    in_hbm = pl.BlockSpec(memory_space=pl.ANY)
     return pl.pallas_call(
         body,
-        grid_spec=pltpu.PrefetchScalarGridSpec(
-            num_scalar_prefetch=1,
-            grid=(1,),
-            in_specs=[
-                whole(tokens),
-                pl.BlockSpec((1, routed), lambda i, c: (0, 0)),
-                pl.BlockSpec((1, routed), lambda i, c: (0, 0)),
-                whole(cotan),
-            ],
-            out_specs=[
-                pl.BlockSpec((2, routed, width), lambda i, c: (0, 0, 0)),
-                pl.BlockSpec(memory_space=pltpu.SMEM),
-            ],
-        ),
-        out_shape=[jax.ShapeDtypeStruct((2, routed, width), BF16), jax.ShapeDtypeStruct((2,), jnp.int32)],
-        compiler_params=params(60),
+        in_specs=[IN_SMEM] + [in_hbm] * 4,
+        out_specs=[IN_VMEM, IN_SMEM],
+        out_shape=[pltpu.VMEM((2, routed, width), BF16), jax.ShapeDtypeStruct((2,), jnp.int32)],
+        scratch_shapes=[
+            pltpu.VMEM((parts, n_tok, part), BF16),
+            pltpu.VMEM((routed, width), BF16),
+            pltpu.VMEM((1, routed), jnp.int32),
+            pltpu.VMEM((1, routed), F32),
+            pltpu.SemaphoreType.DMA((parts + 3,)),
+        ],
+        compiler_params=params(12),
         cost_estimate=LITTLE,
         name="take_rows",
-    )(counts, tokens, picks[None, :], score[None, :], cotan)
-
-
-IN_VMEM = pl.BlockSpec(memory_space=pltpu.VMEM)
-IN_SMEM = pl.BlockSpec(memory_space=pltpu.SMEM)
+    )(
+        counts,
+        *[pltpu.with_memory_space_constraint(a, pltpu.HBM) for a in (picks[None, :], score[None, :], tokens, cotan)],
+    )
 
 
 def held(a):
@@ -337,14 +354,13 @@
 
     return pl.pallas_call(
         body,
-        grid=(1,),
-        in_specs=[whole(a) for a in flat],
-        out_specs=[whole(g[0]) for g in groups],
+        in_specs=[IN_VMEM] * len(flat),
+        out_specs=[IN_VMEM] * len(groups),
         out_shape=[jax.ShapeDtypeStruct(g[0].shape, F32) for g in groups],
         compiler_params=params(10),
         cost_estimate=LITTLE,
         name="add_up",
-    )(*flat)
+    )(*[held(a) for a in flat])
 
 
 def after(values, *deps):

time: 131 us -> 130 us (level)
  transfers between devices with their start and end apart: 28 -> 28, of which waited for: 17 -> 17; matrix products, arithmetic and copies ran while one was open for 5% -> 5% of each run, Pallas kernels for 29% -> 30%
where the time goes in v1:
time: 130 us
  waiting for transfers between devices  49.3 us (38%)
  Pallas kernels  47.3 us (36%)
  starting transfers between devices  24.9 us (19%)
  other arithmetic  4.29 us (3%)
  matrix products  2.14 us (2%)
  between operations  1.57 us (1%)
    pallas_call x12, Pallas kernels, on_held(): pl.pallas_call(body, in_specs=[IN_SMEM] * len(first) + [IN_VMEM] * len(ar...  38.1 us
    ppermute x7, waiting for transfers between devices, move_x(): return lax.ppermute(v, 'ctx', perm)  20 us
    ppermute x5, waiting for transfers between devices, move_lane(): return lax.ppermute(v, 'head', perm)  14.7 us
    ppermute x7, waiting for transfers between devices, move_y(): return lax.ppermute(v, 'ctx', perm)  12.2 us
    ppermute x7, starting transfers between devices, move_y(): return lax.ppermute(v, 'ctx', perm)  9.47 us
    ppermute x7, starting transfers between devices, move_x(): return lax.ppermute(v, 'ctx', perm)  7.62 us
    ppermute x5, starting transfers between devices, move_lane(): return lax.ppermute(v, 'head', perm)  5.67 us
    pallas_call x1, Pallas kernels, hold(): pl.pallas_call(body, in_specs=[pl.BlockSpec(memory_space=pl.ANY)] * 2, ou...  3.48 us
  transfers between devices with their start and end apart: 28, of which 17 were waited for; matrix products, arithmetic and copies ran while one was open for 5% of the time, Pallas kernels for 30%

profile of v1, /device:TPU:70, one launch (start us, length us, event | category | flops | bytes accessed | tf_op | source)
XLA Modules:
  0.0 129.8 jit_solution(6140810696361381292)
XLA Ops:
  1.3 2.4 %take_rows.1 = (bf16[2,128,2048]{2,1,0:T(8,128)(2,1)S(1)}, s32[2]{0:T(128)S(1)}) custom-call(s32[1]{0:T(128)S(6)} %copy.20.counts_ref, s32[1,128]{1,0:T(1,128)} %bitcast.31, f32[1,128]{1,0:T(1,128)} %bitcast.30, bf16[512,2048]{1,0:T(8,128)(2,1)} %tokens_ref.1, bf16[128,2048]{1,0:T(8,128)(2,1)} %cotan_ref.1), custom_call_target="tpu_custom_call" | custom-call | flops 1 | bytes 1 | tf_op jit(solution)/shard_map/take_rows/pallas_call | solution.py:97
  8.0 3.5 %hold_weights.1 = (bf16[2048,1024]{1,0:T(8,128)(2,1)S(1)}, bf16[1024,2048]{1,0:T(8,128)(2,1)S(1)}) custom-call(bf16[2048,1024]{1,0:T(8,128)(2,1)} %win_ref, bf16[1024,2048]{1,0:T(8,128)(2,1)} %wout_ref), custom_call_target="tpu_custom_call" | custom-call | flops 1 | bytes 1 | tf_op jit(solution)/shard_map/hold_weights/pallas_call | solution.py:198
  11.5 3.8 %hidden_units.4 = (bf16[256,1024]{1,0:T(8,128)(2,1)S(1)}, bf16[256,1024]{1,0:T(8,128)(2,1)S(1)}, bf16[256,2048]{1,0:T(8,128)(2,1)S(1)}) custom-call(bf16[2,128,2048]{2,1,0:T(8,128)(2,1)S(1)} %get-tuple-element.183.refs_0_, bf16[2,128,2048]{2,1,0:T(8,128)(2,1)S(1)} %collective-permute-done.refs_1_, ...), custom_call_target="tpu_custom_call" | custom-call | flops 1 | bytes 1 | tf_op jit(solution)/shard_map/hidden_units/pallas_call | solution.py:124
  15.3 3.3 %collective-permute-done.2.refs_0_.refs_2_ = bf16[2,128,2048]{2,1,0:T(8,128)(2,1)S(1)} collective-permute-done((bf16[2,128,2048]{2,1,0:T(8,128)(2,1)S(1)}, bf16[2,128,2048]{2,1,0:T(8,128)(2,1)S(1)}, u32[]{:S(2)}, u32[]{:S(2)}) %collective-permute-start.2) | collective-permute-done | bytes 1048608 | tf_op jit(solution)/shard_map/ppermute | solution.py:39
  19.3 2.8 %row_terms.4 = (bf16[1,2,128,2048]{3,2,1,0:T(8,128)(2,1)S(1)}, bf16[1,2,128,2048]{3,2,1,0:T(8,128)(2,1)S(1)}) custom-call(bf16[256,1024]{1,0:T(8,128)(2,1)S(1)} %get-tuple-element.196.hidden_ref.refs_0_, bf16[256,1024]{1,0:T(8,128)(2,1)S(1)} %get-tuple-element.191.dpre_ref.refs_8_, bf16[2048,1024]{1,0:T(8,128)(2,1)S(1)} %get-tuple-element.124.refs_2_.win_ref.refs_3_, ...), custom_call_target="tpu_custom_call" | custom-call | flops 1 | bytes 1 | tf_op jit(solution)/shard_map/row_terms/pallas_call | solution.py:124
  24.4 3.8 %hidden_units.5 = (bf16[256,1024]{1,0:T(8,128)(2,1)S(1)}, bf16[256,1024]{1,0:T(8,128)(2,1)S(1)}, bf16[256,2048]{1,0:T(8,128)(2,1)S(1)}) custom-call(bf16[2,128,2048]{2,1,0:T(8,128)(2,1)S(1)} %collective-permute-done.2.refs_0_.refs_2_, bf16[1,128,2048]{2,1,0:T(8,128)(2,1)S(1)} %collective-permute-done.3.refs_1_.refs_3_, ...), custom_call_target="tpu_custom_call" | custom-call | flops 1 | bytes 1 | tf_op jit(solution)/shard_map/hidden_units/pallas_call | solution.py:124
  30.6 2.8 %row_terms.5 = (bf16[3,2,128,2048]{3,2,1,0:T(8,128)(2,1)S(1)}, bf16[3,2,128,2048]{3,2,1,0:T(8,128)(2,1)S(1)}) custom-call(bf16[256,1024]{1,0:T(8,128)(2,1)S(1)} %get-tuple-element.197.hidden_ref.refs_1_, bf16[256,1024]{1,0:T(8,128)(2,1)S(1)} %get-tuple-element.192.dpre_ref.refs_9_, bf16[2048,1024]{1,0:T(8,128)(2,1)S(1)} %get-tuple-element.124.refs_2_.win_ref.refs_3_, ...), custom_call_target="tpu_custom_call" | custom-call | flops 1 | bytes 1 | tf_op jit(solution)/shard_map/row_terms/pallas_call | solution.py:124
  33.5 3.8 %hidden_units.6 = (bf16[256,1024]{1,0:T(8,128)(2,1)S(1)}, bf16[256,1024]{1,0:T(8,128)(2,1)S(1)}, bf16[256,2048]{1,0:T(8,128)(2,1)S(1)}) custom-call(bf16[2,128,2048]{2,1,0:T(8,128)(2,1)S(1)} %collective-permute-done.1.refs_0_.refs_4_, bf16[1,128,2048]{2,1,0:T(8,128)(2,1)S(1)} %collective-permute-done.5.refs_1_.refs_5_, ...), custom_call_target="tpu_custom_call" | custom-call | flops 1 | bytes 1 | tf_op jit(solution)/shard_map/hidden_units/pallas_call | solution.py:124
  37.2 3.9 %collective-permute-done.8.refs_0_.refs_6_ = bf16[2,128,2048]{2,1,0:T(8,128)(2,1)S(1)} collective-permute-done((bf16[2,128,2048]{2,1,0:T(8,128)(2,1)S(1)}, bf16[2,128,2048]{2,1,0:T(8,128)(2,1)S(1)}, u32[]{:S(2)}, u32[]{:S(2)}) %collective-permute-start.8) | collective-permute-done | bytes 1048608 | tf_op jit(solution)/shard_map/ppermute | solution.py:39
  41.1 2.8 %row_terms.6 = (bf16[3,2,128,2048]{3,2,1,0:T(8,128)(2,1)S(1)}, bf16[3,2,128,2048]{3,2,1,0:T(8,128)(2,1)S(1)}) custom-call(bf16[256,1024]{1,0:T(8,128)(2,1)S(1)} %get-tuple-element.198.hidden_ref.refs_2_, bf16[256,1024]{1,0:T(8,128)(2,1)S(1)} %get-tuple-element.193.dpre_ref.refs_10_, ...), custom_call_target="tpu_custom_call", output_to_operand_aliasing={{0}: (4, {}), {1}: (5, {})} | custom-call | flops 1 | bytes 1 | tf_op jit(solution)/shard_map/row_terms/pallas_call | solution.py:124
  44.0 2.9 %hidden_units.7 = (bf16[256,1024]{1,0:T(8,128)(2,1)S(1)}, bf16[256,1024]{1,0:T(8,128)(2,1)S(1)}, bf16[256,2048]{1,0:T(8,128)(2,1)S(1)}) custom-call(bf16[2,128,2048]{2,1,0:T(8,128)(2,1)S(1)} %collective-permute-done.8.refs_0_.refs_6_, bf16[2,128,2048]{2,1,0:T(8,128)(2,1)S(1)} %collective-permute-done.9.refs_1_.refs_7_, ...), custom_call_target="tpu_custom_call" | custom-call | flops 1 | bytes 1 | tf_op jit(solution)/shard_map/hidden_units/pallas_call | solution.py:124
  46.8 2.4 %row_terms.7 = (bf16[3,2,128,2048]{3,2,1,0:T(8,128)(2,1)S(1)}, bf16[3,2,128,2048]{3,2,1,0:T(8,128)(2,1)S(1)}) custom-call(bf16[256,1024]{1,0:T(8,128)(2,1)S(1)} %get-tuple-element.199.hidden_ref.refs_3_, bf16[256,1024]{1,0:T(8,128)(2,1)S(1)} %get-tuple-element.194.dpre_ref.refs_11_, ...), custom_call_target="tpu_custom_call", output_to_operand_aliasing={{0}: (4, {}), {1}: (5, {})} | custom-call | flops 1 | bytes 1 | tf_op jit(solution)/shard_map/row_terms/pallas_call | solution.py:124
  49.8 2.9 %in_blocks.2 = (bf16[2,256,1024]{2,1,0:T(8,128)(2,1)S(1)}, bf16[2,256,1024]{2,1,0:T(8,128)(2,1)S(1)}) custom-call(s32[2]{0:T(128)S(1)} %get-tuple-element.156.me_ref, bf16[2,128,2048]{2,1,0:T(8,128)(2,1)S(1)} %get-tuple-element.183.refs_0_, bf16[2,128,2048]{2,1,0:T(8,128)(2,1)S(1)} %collective-permute-done.refs_1_, ...), custom_call_target="tpu_custom_call" | custom-call | flops 1 | bytes 1 | tf_op jit(solution)/shard_map/in_blocks/pallas_call | solution.py:124
  52.8 2.9 %out_blocks.2 = (bf16[2,512,512]{2,1,0:T(8,128)(2,1)S(1)}, bf16[2,512,512]{2,1,0:T(8,128)(2,1)S(1)}) custom-call(s32[2]{0:T(128)S(1)} %get-tuple-element.156.me_ref, bf16[256,1024]{1,0:T(8,128)(2,1)S(1)} %get-tuple-element.196.hidden_ref.refs_0_, bf16[256,1024]{1,0:T(8,128)(2,1)S(1)} %get-tuple-element.197.hidden_ref.refs_1_, ...), custom_call_target="tpu_custom_call" | custom-call | flops 1 | bytes 1 | tf_op jit(solution)/shard_map/out_blocks/pallas_call | solution.py:124
  61.6 3.6 %in_blocks.3.later_ref = bf16[4,256,1024]{2,1,0:T(8,128)(2,1)S(1)} custom-call(s32[2]{0:T(128)S(1)} %get-tuple-element.156.me_ref, bf16[2,128,2048]{2,1,0:T(8,128)(2,1)S(1)} %get-tuple-element.183.refs_0_, bf16[2,128,2048]{2,1,0:T(8,128)(2,1)S(1)} %collective-permute-done.refs_1_, bf16[2,128,2048]{2,1,0:T(8,128)(2,1)S(1)} %collective-permute-done.2.refs_0_.refs_2_, ...), custom_call_target="tpu_custom_call" | custom-call | flops 1 | bytes 1 | tf_op jit(solution)/shard_map/in_blocks/pallas_call | solution.py:124
  65.2 5.8 %collective-permute-done.11 = bf16[2,128,2048]{2,1,0:T(8,128)(2,1)S(1)} collective-permute-done((bf16[2,128,2048]{2,1,0:T(8,128)(2,1)S(1)}, bf16[2,128,2048]{2,1,0:T(8,128)(2,1)S(1)}, u32[]{:S(2)}, u32[]{:S(2)}) %collective-permute-start.11) | collective-permute-done | bytes 1048608 | tf_op jit(solution)/shard_map/ppermute | solution.py:39
  72.2 3.5 %out_blocks.3.later_ref = bf16[4,512,512]{2,1,0:T(8,128)(2,1)S(1)} custom-call(s32[2]{0:T(128)S(1)} %get-tuple-element.156.me_ref, bf16[256,1024]{1,0:T(8,128)(2,1)S(1)} %get-tuple-element.196.hidden_ref.refs_0_, bf16[256,1024]{1,0:T(8,128)(2,1)S(1)} %get-tuple-element.197.hidden_ref.refs_1_, bf16[256,1024]{1,0:T(8,128)(2,1)S(1)} %get-tuple-element.198.hidden_ref.refs_2_, ...), custom_call_target="tpu_custom_call" | custom-call | flops 1 | bytes 1 | tf_op jit(solution)/shard_map/out_blocks/pallas_call | solution.py:124
  75.7 5.9 %collective-permute-done.13.b1 = bf16[2,256,1024]{2,1,0:T(8,128)(2,1)S(1)} collective-permute-done((bf16[2,256,1024]{2,1,0:T(8,128)(2,1)S(1)}, bf16[2,256,1024]{2,1,0:T(8,128)(2,1)S(1)}, u32[]{:S(2)}, u32[]{:S(2)}) %collective-permute-start.13) | collective-permute-done | bytes 1048608 | tf_op jit(solution)/shard_map/ppermute | solution.py:29
  87.1 2.4 %collective-permute-start.17 = (bf16[256,1024]{1,0:T(8,128)(2,1)S(1)}, bf16[256,1024]{1,0:T(8,128)(2,1)S(1)}, u32[]{:S(2)}, u32[]{:S(2)}) collective-permute-start(bf16[256,1024]{1,0:T(8,128)(2,1)S(1)} %get-tuple-element.240), channel_id=1, source_target_pairs={{0,32},{8,40},{16,48},{24,56},{32,64},{40,72},{48,80},{56,88},{64,... | collective-permute-start | bytes 1572872 | tf_op jit(solution)/shard_map/ppermute | solution.py:29
  89.8 3.0 %collective-permute-start.20 = (bf16[512,512]{1,0:T(8,128)(2,1)S(1)}, bf16[512,512]{1,0:T(8,128)(2,1)S(1)}, u32[]{:S(2)}, u32[]{:S(2)}) collective-permute-start(bf16[512,512]{1,0:T(8,128)(2,1)S(1)} %get-tuple-element.237), channel_id=1, source_target_pairs={{0,24},{8,0},{16,8},{24,16},{32,56},{40,32},{48,40},{56,48},{64,88... | collective-permute-start | bytes 1572872 | tf_op jit(solution)/shard_map/ppermute | solution.py:34
  92.8 8.5 %collective-permute-done.18.a1 = bf16[256,1024]{1,0:T(8,128)(2,1)S(1)} collective-permute-done((bf16[256,1024]{1,0:T(8,128)(2,1)S(1)}, bf16[256,1024]{1,0:T(8,128)(2,1)S(1)}, u32[]{:S(2)}, u32[]{:S(2)}) %collective-permute-start.18) | collective-permute-done | bytes 524320 | tf_op jit(solution)/shard_map/ppermute | solution.py:29
  103.7 3.4 %collective-permute-done.19.b0 = bf16[512,512]{1,0:T(8,128)(2,1)S(1)} collective-permute-done((bf16[512,512]{1,0:T(8,128)(2,1)S(1)}, bf16[512,512]{1,0:T(8,128)(2,1)S(1)}, u32[]{:S(2)}, u32[]{:S(2)}) %collective-permute-start.19) | collective-permute-done | bytes 524320 | tf_op jit(solution)/shard_map/ppermute | solution.py:34
  122.2 2.9 %collective-permute-done.23.refs_2_ = bf16[128,1024]{1,0:T(8,128)(2,1)S(1)} collective-permute-done((bf16[128,1024]{1,0:T(8,128)(2,1)S(1)}, bf16[128,1024]{1,0:T(8,128)(2,1)S(1)}, u32[]{:S(2)}, u32[]{:S(2)}) %collective-permute-start.23) | collective-permute-done | bytes 262176 | tf_op jit(solution)/shard_map/ppermute | solution.py:34
  126.3 2.4 %collective-permute-done.27.refs_7_ = bf16[1024,128]{1,0:T(8,128)(2,1)S(1)} collective-permute-done((bf16[1024,128]{1,0:T(8,128)(2,1)S(1)}, bf16[1024,128]{1,0:T(8,128)(2,1)S(1)}, u32[]{:S(2)}, u32[]{:S(2)}) %collective-permute-start.27) | collective-permute-done | bytes 262176 | tf_op jit(solution)/shard_map/ppermute | solution.py:29
  (65 shorter events, 42.6 us)
Async XLA Ops:
  3.8 14.9 %collective-permute-start.2 = (bf16[2,128,2048]{2,1,0:T(8,128)(2,1)S(1)}, bf16[2,128,2048]{2,1,0:T(8,128)(2,1)S(1)}, u32[]{:S(2)}, u32[]{:S(2)}) collective-permute-start(bf16[2,128,2048]{2,1,0:T(8,128)(2,1)S(1)} %get-tuple-element.183.refs_0_), channel_id=1, source_target_pairs={{0,2},{1,7},{2,4},{3,1},{4,6},{5,3},{6,0},{7,5},{8,10},{9,15},{10,... | collective-permute-start | bytes 3145736 | tf_op jit(solution)/shard_map/ppermute | solution.py:39
  6.4 23.5 %collective-permute-start.1 = (bf16[2,128,2048]{2,1,0:T(8,128)(2,1)S(1)}, bf16[2,128,2048]{2,1,0:T(8,128)(2,1)S(1)}, u32[]{:S(2)}, u32[]{:S(2)}) collective-permute-start(bf16[2,128,2048]{2,1,0:T(8,128)(2,1)S(1)} %collective-permute-done.refs_1_), channel_id=1, source_target_pairs={{0,2},{1,7},{2,4},{3,1},{4,6},{5,3},{6,0},{7,5},{8,10},{9,15},{10,... | collective-permute-start | bytes 3145736 | tf_op jit(solution)/shard_map/ppermute | solution.py:39
  18.7 5.6 %collective-permute-start.4 = (bf16[1,128,2048]{2,1,0:T(8,128)(2,1)S(1)}, bf16[1,128,2048]{2,1,0:T(8,128)(2,1)S(1)}, u32[]{:S(2)}, u32[]{:S(2)}) collective-permute-start(bf16[1,128,2048]{2,1,0:T(8,128)(2,1)S(1)} %get-tuple-element.245), channel_id=1, source_target_pairs={{0,1},{1,0},{2,3},{3,2},{4,5},{5,4},{6,7},{7,6},{8,9},{9,8},{10,11... | collective-permute-start | bytes 1572872 | tf_op jit(solution)/shard_map/ppermute | solution.py:43
  18.8 5.5 %collective-permute-start.3 = (bf16[1,128,2048]{2,1,0:T(8,128)(2,1)S(1)}, bf16[1,128,2048]{2,1,0:T(8,128)(2,1)S(1)}, u32[]{:S(2)}, u32[]{:S(2)}) collective-permute-start(bf16[1,128,2048]{2,1,0:T(8,128)(2,1)S(1)} %get-tuple-element.246), channel_id=1, source_target_pairs={{0,1},{1,0},{2,3},{3,2},{4,5},{5,4},{6,7},{7,6},{8,9},{9,8},{10,11... | collective-permute-start | bytes 1572872 | tf_op jit(solution)/shard_map/ppermute | solution.py:43
  22.2 11.2 %collective-permute-start.7 = (bf16[1,2,128,2048]{3,2,1,0:T(8,128)(2,1)S(1)}, bf16[1,2,128,2048]{3,2,1,0:T(8,128)(2,1)S(1)}, u32[]{:S(2)}, u32[]{:S(2)}) collective-permute-start(bf16[1,2,128,2048]{3,2,1,0:T(8,128)(2,1)S(1)} %get-tuple-element.131), channel_id=1, source_target_pairs={{0,1},{1,0},{2,3},{3,2},{4,5},{5,4},{6,7},{7,6},{8,9},{9,8},{10,11... | collective-permute-start | bytes 3145736 | tf_op jit(solution)/shard_map/ppermute | solution.py:43
  22.4 18.7 %collective-permute-start.8 = (bf16[2,128,2048]{2,1,0:T(8,128)(2,1)S(1)}, bf16[2,128,2048]{2,1,0:T(8,128)(2,1)S(1)}, u32[]{:S(2)}, u32[]{:S(2)}) collective-permute-start(bf16[2,128,2048]{2,1,0:T(8,128)(2,1)S(1)} %collective-permute-done.2.refs_0_.refs_2_), channel_id=1, source_target_pairs={{0,2},{1,7},{2,4},{3,1},{4,6},{5,3},{6,0},{7,5},{8,10},{9,15},{10,... | collective-permute-start | bytes 3145736 | tf_op jit(solution)/shard_map/ppermute | solution.py:39
  30.0 3.5 %collective-permute-start.6 = (bf16[1,128,2048]{2,1,0:T(8,128)(2,1)S(1)}, bf16[1,128,2048]{2,1,0:T(8,128)(2,1)S(1)}, u32[]{:S(2)}, u32[]{:S(2)}) collective-permute-start(bf16[1,128,2048]{2,1,0:T(8,128)(2,1)S(1)} %get-tuple-element.243), channel_id=1, source_target_pairs={{0,1},{1,0},{2,3},{3,2},{4,5},{5,4},{6,7},{7,6},{8,9},{9,8},{10,11... | collective-permute-start | bytes 1572872 | tf_op jit(solution)/shard_map/ppermute | solution.py:43
  49.2 6.5 %collective-permute-start.10 = (bf16[3,2,128,2048]{3,2,1,0:T(8,128)(2,1)S(1)}, bf16[3,2,128,2048]{3,2,1,0:T(8,128)(2,1)S(1)}, u32[]{:S(2)}, u32[]{:S(2)}) collective-permute-start(bf16[3,2,128,2048]{3,2,1,0:T(8,128)(2,1)S(1)} %get-tuple-element.155), channel_id=1, source_target_pairs={{0,1},{1,0},{2,3},{3,2},{4,5},{5,4},{6,7},{7,6},{8,9},{9,8},{10,11... | collective-permute-start | bytes 9437192 | tf_op jit(solution)/shard_map/ppermute | solution.py:43
  56.1 14.9 %collective-permute-start.11 = (bf16[2,128,2048]{2,1,0:T(8,128)(2,1)S(1)}, bf16[2,128,2048]{2,1,0:T(8,128)(2,1)S(1)}, u32[]{:S(2)}, u32[]{:S(2)}) collective-permute-start(bf16[2,128,2048]{2,1,0:T(8,128)(2,1)S(1)} %fusion.3), channel_id=1, source_target_pairs={{0,6},{1,3},{2,0},{3,5},{4,2},{5,7},{6,4},{7,1},{8,14},{9,11},{10,... | collective-permute-start | bytes 3145736 | tf_op jit(solution)/shard_map/ppermute | solution.py:39
  56.3 25.3 %collective-permute-start.13 = (bf16[2,256,1024]{2,1,0:T(8,128)(2,1)S(1)}, bf16[2,256,1024]{2,1,0:T(8,128)(2,1)S(1)}, u32[]{:S(2)}, u32[]{:S(2)}) collective-permute-start(bf16[2,256,1024]{2,1,0:T(8,128)(2,1)S(1)} %get-tuple-element.170), channel_id=1, source_target_pairs={{0,32},{8,40},{16,48},{24,56},{32,64},{40,72},{48,80},{56,88},{64,... | collective-permute-start | bytes 3145736 | tf_op jit(solution)/shard_map/ppermute | solution.py:29
  56.7 26.8 %collective-permute-start.14 = (bf16[2,256,1024]{2,1,0:T(8,128)(2,1)S(1)}, bf16[2,256,1024]{2,1,0:T(8,128)(2,1)S(1)}, u32[]{:S(2)}, u32[]{:S(2)}) collective-permute-start(bf16[2,256,1024]{2,1,0:T(8,128)(2,1)S(1)} %get-tuple-element.171), channel_id=1, source_target_pairs={{0,96},{8,104},{16,112},{24,120},{32,0},{40,8},{48,16},{56,24},{64... | collective-permute-start | bytes 3145736 | tf_op jit(solution)/shard_map/ppermute | solution.py:29
  58.3 27.0 %collective-permute-start.15 = (bf16[2,512,512]{2,1,0:T(8,128)(2,1)S(1)}, bf16[2,512,512]{2,1,0:T(8,128)(2,1)S(1)}, u32[]{:S(2)}, u32[]{:S(2)}) collective-permute-start(bf16[2,512,512]{2,1,0:T(8,128)(2,1)S(1)} %get-tuple-element.180), channel_id=1, source_target_pairs={{0,8},{8,16},{16,24},{24,0},{32,40},{40,48},{48,56},{56,32},{64,72... | collective-permute-start | bytes 3145736 | tf_op jit(solution)/shard_map/ppermute | solution.py:34
  59.9 25.9 %collective-permute-start.16 = (bf16[2,512,512]{2,1,0:T(8,128)(2,1)S(1)}, bf16[2,512,512]{2,1,0:T(8,128)(2,1)S(1)}, u32[]{:S(2)}, u32[]{:S(2)}) collective-permute-start(bf16[2,512,512]{2,1,0:T(8,128)(2,1)S(1)} %get-tuple-element.181), channel_id=1, source_target_pairs={{0,24},{8,0},{16,8},{24,16},{32,56},{40,32},{48,40},{56,48},{64,88... | collective-permute-start | bytes 3145736 | tf_op jit(solution)/shard_map/ppermute | solution.py:34
  72.0 35.1 %collective-permute-start.12 = (bf16[2,2,128,2048]{3,2,1,0:T(8,128)(2,1)S(1)}, bf16[2,2,128,2048]{3,2,1,0:T(8,128)(2,1)S(1)}, u32[]{:S(2)}, u32[]{:S(2)}) collective-permute-start(bf16[2,2,128,2048]{3,2,1,0:T(8,128)(2,1)S(1)} %add_convert_fusion), channel_id=1, source_target_pairs={{0,6},{1,3},{2,0},{3,5},{4,2},{5,7},{6,4},{7,1},{8,14},{9,11},{10,... | collective-permute-start | bytes 6291464 | tf_op jit(solution)/shard_map/ppermute | solution.py:39
  86.2 15.1 %collective-permute-start.18 = (bf16[256,1024]{1,0:T(8,128)(2,1)S(1)}, bf16[256,1024]{1,0:T(8,128)(2,1)S(1)}, u32[]{:S(2)}, u32[]{:S(2)}) collective-permute-start(bf16[256,1024]{1,0:T(8,128)(2,1)S(1)} %get-tuple-element.239), channel_id=1, source_target_pairs={{0,96},{8,104},{16,112},{24,120},{32,0},{40,8},{48,16},{56,24},{64... | collective-permute-start | bytes 1572872 | tf_op jit(solution)/shard_map/ppermute | solution.py:29
  87.1 14.3 %collective-permute-start.17 = (bf16[256,1024]{1,0:T(8,128)(2,1)S(1)}, bf16[256,1024]{1,0:T(8,128)(2,1)S(1)}, u32[]{:S(2)}, u32[]{:S(2)}) collective-permute-start(bf16[256,1024]{1,0:T(8,128)(2,1)S(1)} %get-tuple-element.240), channel_id=1, source_target_pairs={{0,32},{8,40},{16,48},{24,56},{32,64},{40,72},{48,80},{56,88},{64,... | collective-permute-start | bytes 1572872 | tf_op jit(solution)/shard_map/ppermute | solution.py:29
  89.8 13.9 %collective-permute-start.20 = (bf16[512,512]{1,0:T(8,128)(2,1)S(1)}, bf16[512,512]{1,0:T(8,128)(2,1)S(1)}, u32[]{:S(2)}, u32[]{:S(2)}) collective-permute-start(bf16[512,512]{1,0:T(8,128)(2,1)S(1)} %get-tuple-element.237), channel_id=1, source_target_pairs={{0,24},{8,0},{16,8},{24,16},{32,56},{40,32},{48,40},{56,48},{64,88... | collective-permute-start | bytes 1572872 | tf_op jit(solution)/shard_map/ppermute | solution.py:34
  92.8 14.3 %collective-permute-start.19 = (bf16[512,512]{1,0:T(8,128)(2,1)S(1)}, bf16[512,512]{1,0:T(8,128)(2,1)S(1)}, u32[]{:S(2)}, u32[]{:S(2)}) collective-permute-start(bf16[512,512]{1,0:T(8,128)(2,1)S(1)} %get-tuple-element.238), channel_id=1, source_target_pairs={{0,8},{8,16},{16,24},{24,0},{32,40},{40,48},{48,56},{56,32},{64,72... | collective-permute-start | bytes 1572872 | tf_op jit(solution)/shard_map/ppermute | solution.py:34
  109.9 10.7 %collective-permute-start.22 = (bf16[128,1024]{1,0:T(8,128)(2,1)S(1)}, bf16[128,1024]{1,0:T(8,128)(2,1)S(1)}, u32[]{:S(2)}, u32[]{:S(2)}) collective-permute-start(bf16[128,1024]{1,0:T(8,128)(2,1)S(1)} %get-tuple-element.220), channel_id=1, source_target_pairs={{0,16},{8,24},{16,0},{24,8},{32,48},{40,56},{48,32},{56,40},{64,80... | collective-permute-start | bytes 786440 | tf_op jit(solution)/shard_map/ppermute | solution.py:34
  109.9 15.2 %collective-permute-start.23 = (bf16[128,1024]{1,0:T(8,128)(2,1)S(1)}, bf16[128,1024]{1,0:T(8,128)(2,1)S(1)}, u32[]{:S(2)}, u32[]{:S(2)}) collective-permute-start(bf16[128,1024]{1,0:T(8,128)(2,1)S(1)} %get-tuple-element.221), channel_id=1, source_target_pairs={{0,8},{8,16},{16,24},{24,0},{32,40},{40,48},{48,56},{56,32},{64,72... | collective-permute-start | bytes 786440 | tf_op jit(solution)/shard_map/ppermute | solution.py:34
  111.0 14.0 %collective-permute-start.24 = (bf16[128,1024]{1,0:T(8,128)(2,1)S(1)}, bf16[128,1024]{1,0:T(8,128)(2,1)S(1)}, u32[]{:S(2)}, u32[]{:S(2)}) collective-permute-start(bf16[128,1024]{1,0:T(8,128)(2,1)S(1)} %get-tuple-element.222), channel_id=1, source_target_pairs={{0,24},{8,0},{16,8},{24,16},{32,56},{40,32},{48,40},{56,48},{64,88... | collective-permute-start | bytes 786440 | tf_op jit(solution)/shard_map/ppermute | solution.py:34
  113.1 11.9 %collective-permute-start.25 = (bf16[1024,128]{1,0:T(8,128)(2,1)S(1)}, bf16[1024,128]{1,0:T(8,128)(2,1)S(1)}, u32[]{:S(2)}, u32[]{:S(2)}) collective-permute-start(bf16[1024,128]{1,0:T(8,128)(2,1)S(1)} %get-tuple-element.224), channel_id=1, source_target_pairs={{0,64},{8,72},{16,80},{24,88},{32,96},{40,104},{48,112},{56,120},{... | collective-permute-start | bytes 786440 | tf_op jit(solution)/shard_map/ppermute | solution.py:29
  113.4 12.9 %collective-permute-start.26 = (bf16[1024,128]{1,0:T(8,128)(2,1)S(1)}, bf16[1024,128]{1,0:T(8,128)(2,1)S(1)}, u32[]{:S(2)}, u32[]{:S(2)}) collective-permute-start(bf16[1024,128]{1,0:T(8,128)(2,1)S(1)} %get-tuple-element.225), channel_id=1, source_target_pairs={{0,32},{8,40},{16,48},{24,56},{32,64},{40,72},{48,80},{56,88},{64,... | collective-permute-start | bytes 786440 | tf_op jit(solution)/shard_map/ppermute | solution.py:29
  120.6 8.1 %collective-permute-start.27 = (bf16[1024,128]{1,0:T(8,128)(2,1)S(1)}, bf16[1024,128]{1,0:T(8,128)(2,1)S(1)}, u32[]{:S(2)}, u32[]{:S(2)}) collective-permute-start(bf16[1024,128]{1,0:T(8,128)(2,1)S(1)} %get-tuple-element.226), channel_id=1, source_target_pairs={{0,96},{8,104},{16,112},{24,120},{32,0},{40,8},{48,16},{56,24},{64... | collective-permute-start | bytes 786440 | tf_op jit(solution)/shard_map/ppermute | solution.py:29
  (7 other events, 26.9 us)

commit v2 on v1

--- a/solution.py
+++ b/solution.py
@@ -393,8 +393,8 @@
     other = hidden_units([[near_other], swapped_other], w_in, w_out)
     near_terms = row_terms(other[0], other[1], w_in, w_out, routed, 3, 1, near_terms)
 
-    far_mine = after(far_mine, other)
-    far_packs = after([far_mine, swap_core(far_mine)], near_terms)
+    far_mine = after(far_mine, near_terms)
+    far_packs = [far_mine, swap_core(far_mine)]
     far = hidden_units([[p] for p in far_packs], w_in, w_out, True)
     last_terms = row_terms(far[0], far[1], w_in, w_out, routed, 3, 2, near_terms, True)
     last_got = swap_core(last_terms[1])

time: 130 us -> 129 us (level)
    ppermute x5, waiting for transfers between devices: 14.7 us -> 11.8 us  [move_lane(): return lax.ppermute(v, 'head', perm)]
    ppermute x9, waiting for transfers between devices: 2.43 us -> 5.08 us  [swap_core(): return lax.ppermute(v, 'head', [(i, i ^ 1) for i in range(2 * SIDE)])]
  transfers between devices with their start and end apart: 28 -> 28, of which waited for: 17 -> 18; matrix products, arithmetic and copies ran while one was open for 5% -> 5% of each run, Pallas kernels for 30% -> 30%
where the time goes in v2:
time: 129 us
  waiting for transfers between devices  48.9 us (38%)
  Pallas kernels  47.3 us (37%)
  starting transfers between devices  24.7 us (19%)
  other arithmetic  4.29 us (3%)
  matrix products  2.14 us (2%)
  between operations  1.56 us (1%)
    pallas_call x12, Pallas kernels, on_held(): pl.pallas_call(body, in_specs=[IN_SMEM] * len(first) + [IN_VMEM] * len(ar...  38.1 us
    ppermute x7, waiting for transfers between devices, move_x(): return lax.ppermute(v, 'ctx', perm)  19.8 us
    ppermute x7, waiting for transfers between devices, move_y(): return lax.ppermute(v, 'ctx', perm)  12.2 us
    ppermute x5, waiting for transfers between devices, move_lane(): return lax.ppermute(v, 'head', perm)  11.8 us
    ppermute x7, starting transfers between devices, move_y(): return lax.ppermute(v, 'ctx', perm)  9.46 us
    ppermute x7, starting transfers between devices, move_x(): return lax.ppermute(v, 'ctx', perm)  7.62 us
    ppermute x5, starting transfers between devices, move_lane(): return lax.ppermute(v, 'head', perm)  5.95 us
    ppermute x9, waiting for transfers between devices, swap_core(): return lax.ppermute(v, 'head', [(i, i ^ 1) for i in range(2 * SIDE)])  5.08 us
  transfers between devices with their start and end apart: 28, of which 18 were waited for; matrix products, arithmetic and copies ran while one was open for 5% of the time, Pallas kernels for 30%

profile of v2, /device:TPU:70, one launch (start us, length us, event | category | flops | bytes accessed | tf_op | source)
XLA Modules:
  0.0 129.2 jit_solution(7451348313936191140)
XLA Ops:
  1.3 2.4 %take_rows.1 = (bf16[2,128,2048]{2,1,0:T(8,128)(2,1)S(1)}, s32[2]{0:T(128)S(1)}) custom-call(s32[1]{0:T(128)S(6)} %copy.20.counts_ref, s32[1,128]{1,0:T(1,128)} %bitcast.31, f32[1,128]{1,0:T(1,128)} %bitcast.30, bf16[512,2048]{1,0:T(8,128)(2,1)} %tokens_ref.1, bf16[128,2048]{1,0:T(8,128)(2,1)} %cotan_ref.1), custom_call_target="tpu_custom_call" | custom-call | flops 1 | bytes 1 | tf_op jit(solution)/shard_map/take_rows/pallas_call | solution.py:97
  8.0 3.5 %hold_weights.1 = (bf16[2048,1024]{1,0:T(8,128)(2,1)S(1)}, bf16[1024,2048]{1,0:T(8,128)(2,1)S(1)}) custom-call(bf16[2048,1024]{1,0:T(8,128)(2,1)} %win_ref, bf16[1024,2048]{1,0:T(8,128)(2,1)} %wout_ref), custom_call_target="tpu_custom_call" | custom-call | flops 1 | bytes 1 | tf_op jit(solution)/shard_map/hold_weights/pallas_call | solution.py:198
  11.5 3.8 %hidden_units.4 = (bf16[256,1024]{1,0:T(8,128)(2,1)S(1)}, bf16[256,1024]{1,0:T(8,128)(2,1)S(1)}, bf16[256,2048]{1,0:T(8,128)(2,1)S(1)}) custom-call(bf16[2,128,2048]{2,1,0:T(8,128)(2,1)S(1)} %get-tuple-element.179.refs_0_, bf16[2,128,2048]{2,1,0:T(8,128)(2,1)S(1)} %collective-permute-done.refs_1_, ...), custom_call_target="tpu_custom_call" | custom-call | flops 1 | bytes 1 | tf_op jit(solution)/shard_map/hidden_units/pallas_call | solution.py:124
  15.3 3.3 %collective-permute-done.2.refs_0_.refs_2_ = bf16[2,128,2048]{2,1,0:T(8,128)(2,1)S(1)} collective-permute-done((bf16[2,128,2048]{2,1,0:T(8,128)(2,1)S(1)}, bf16[2,128,2048]{2,1,0:T(8,128)(2,1)S(1)}, u32[]{:S(2)}, u32[]{:S(2)}) %collective-permute-start.2) | collective-permute-done | bytes 1048608 | tf_op jit(solution)/shard_map/ppermute | solution.py:39
  19.3 2.8 %row_terms.4 = (bf16[1,2,128,2048]{3,2,1,0:T(8,128)(2,1)S(1)}, bf16[1,2,128,2048]{3,2,1,0:T(8,128)(2,1)S(1)}) custom-call(bf16[256,1024]{1,0:T(8,128)(2,1)S(1)} %get-tuple-element.192.hidden_ref.refs_0_, bf16[256,1024]{1,0:T(8,128)(2,1)S(1)} %get-tuple-element.187.dpre_ref.refs_8_, bf16[2048,1024]{1,0:T(8,128)(2,1)S(1)} %get-tuple-element.122.refs_2_.win_ref.refs_3_, ...), custom_call_target="tpu_custom_call" | custom-call | flops 1 | bytes 1 | tf_op jit(solution)/shard_map/row_terms/pallas_call | solution.py:124
  24.4 3.8 %hidden_units.5 = (bf16[256,1024]{1,0:T(8,128)(2,1)S(1)}, bf16[256,1024]{1,0:T(8,128)(2,1)S(1)}, bf16[256,2048]{1,0:T(8,128)(2,1)S(1)}) custom-call(bf16[2,128,2048]{2,1,0:T(8,128)(2,1)S(1)} %collective-permute-done.2.refs_0_.refs_2_, bf16[1,128,2048]{2,1,0:T(8,128)(2,1)S(1)} %collective-permute-done.3.refs_1_.refs_3_, ...), custom_call_target="tpu_custom_call" | custom-call | flops 1 | bytes 1 | tf_op jit(solution)/shard_map/hidden_units/pallas_call | solution.py:124
  30.6 2.8 %row_terms.5 = (bf16[3,2,128,2048]{3,2,1,0:T(8,128)(2,1)S(1)}, bf16[3,2,128,2048]{3,2,1,0:T(8,128)(2,1)S(1)}) custom-call(bf16[256,1024]{1,0:T(8,128)(2,1)S(1)} %get-tuple-element.193.hidden_ref.refs_1_, bf16[256,1024]{1,0:T(8,128)(2,1)S(1)} %get-tuple-element.188.dpre_ref.refs_9_, bf16[2048,1024]{1,0:T(8,128)(2,1)S(1)} %get-tuple-element.122.refs_2_.win_ref.refs_3_, ...), custom_call_target="tpu_custom_call" | custom-call | flops 1 | bytes 1 | tf_op jit(solution)/shard_map/row_terms/pallas_call | solution.py:124
  33.5 3.8 %hidden_units.6 = (bf16[256,1024]{1,0:T(8,128)(2,1)S(1)}, bf16[256,1024]{1,0:T(8,128)(2,1)S(1)}, bf16[256,2048]{1,0:T(8,128)(2,1)S(1)}) custom-call(bf16[2,128,2048]{2,1,0:T(8,128)(2,1)S(1)} %collective-permute-done.1.refs_0_.refs_4_, bf16[1,128,2048]{2,1,0:T(8,128)(2,1)S(1)} %collective-permute-done.5.refs_1_.refs_5_, ...), custom_call_target="tpu_custom_call" | custom-call | flops 1 | bytes 1 | tf_op jit(solution)/shard_map/hidden_units/pallas_call | solution.py:124
  37.2 2.9 %row_terms.6 = (bf16[3,2,128,2048]{3,2,1,0:T(8,128)(2,1)S(1)}, bf16[3,2,128,2048]{3,2,1,0:T(8,128)(2,1)S(1)}) custom-call(bf16[256,1024]{1,0:T(8,128)(2,1)S(1)} %get-tuple-element.194.hidden_ref.refs_2_, bf16[256,1024]{1,0:T(8,128)(2,1)S(1)} %get-tuple-element.189.dpre_ref.refs_10_, ...), custom_call_target="tpu_custom_call", output_to_operand_aliasing={{0}: (4, {}), {1}: (5, {})} | custom-call | flops 1 | bytes 1 | tf_op jit(solution)/shard_map/row_terms/pallas_call | solution.py:124
  41.1 2.7 %collective-permute-done.9.refs_1_.refs_7_ = bf16[2,128,2048]{2,1,0:T(8,128)(2,1)S(1)} collective-permute-done((bf16[2,128,2048]{2,1,0:T(8,128)(2,1)S(1)}, bf16[2,128,2048]{2,1,0:T(8,128)(2,1)S(1)}, u32[]{:S(2)}, u32[]{:S(2)}) %collective-permute-start.9) | collective-permute-done | bytes 1048608 | tf_op jit(solution)/shard_map/ppermute | solution.py:43
  43.8 2.9 %hidden_units.7 = (bf16[256,1024]{1,0:T(8,128)(2,1)S(1)}, bf16[256,1024]{1,0:T(8,128)(2,1)S(1)}, bf16[256,2048]{1,0:T(8,128)(2,1)S(1)}) custom-call(bf16[2,128,2048]{2,1,0:T(8,128)(2,1)S(1)} %collective-permute-done.8.refs_0_.refs_6_, bf16[2,128,2048]{2,1,0:T(8,128)(2,1)S(1)} %collective-permute-done.9.refs_1_.refs_7_, ...), custom_call_target="tpu_custom_call" | custom-call | flops 1 | bytes 1 | tf_op jit(solution)/shard_map/hidden_units/pallas_call | solution.py:124
  46.6 2.4 %row_terms.7 = (bf16[3,2,128,2048]{3,2,1,0:T(8,128)(2,1)S(1)}, bf16[3,2,128,2048]{3,2,1,0:T(8,128)(2,1)S(1)}) custom-call(bf16[256,1024]{1,0:T(8,128)(2,1)S(1)} %get-tuple-element.195.hidden_ref.refs_3_, bf16[256,1024]{1,0:T(8,128)(2,1)S(1)} %get-tuple-element.190.dpre_ref.refs_11_, ...), custom_call_target="tpu_custom_call", output_to_operand_aliasing={{0}: (4, {}), {1}: (5, {})} | custom-call | flops 1 | bytes 1 | tf_op jit(solution)/shard_map/row_terms/pallas_call | solution.py:124
  49.2 2.9 %in_blocks.2 = (bf16[2,256,1024]{2,1,0:T(8,128)(2,1)S(1)}, bf16[2,256,1024]{2,1,0:T(8,128)(2,1)S(1)}) custom-call(s32[2]{0:T(128)S(1)} %get-tuple-element.151.me_ref, bf16[2,128,2048]{2,1,0:T(8,128)(2,1)S(1)} %get-tuple-element.179.refs_0_, bf16[2,128,2048]{2,1,0:T(8,128)(2,1)S(1)} %collective-permute-done.refs_1_, ...), custom_call_target="tpu_custom_call" | custom-call | flops 1 | bytes 1 | tf_op jit(solution)/shard_map/in_blocks/pallas_call | solution.py:124
  52.2 2.9 %out_blocks.2 = (bf16[2,512,512]{2,1,0:T(8,128)(2,1)S(1)}, bf16[2,512,512]{2,1,0:T(8,128)(2,1)S(1)}) custom-call(s32[2]{0:T(128)S(1)} %get-tuple-element.151.me_ref, bf16[256,1024]{1,0:T(8,128)(2,1)S(1)} %get-tuple-element.192.hidden_ref.refs_0_, bf16[256,1024]{1,0:T(8,128)(2,1)S(1)} %get-tuple-element.193.hidden_ref.refs_1_, ...), custom_call_target="tpu_custom_call" | custom-call | flops 1 | bytes 1 | tf_op jit(solution)/shard_map/out_blocks/pallas_call | solution.py:124
  61.0 3.6 %in_blocks.3.later_ref = bf16[4,256,1024]{2,1,0:T(8,128)(2,1)S(1)} custom-call(s32[2]{0:T(128)S(1)} %get-tuple-element.151.me_ref, bf16[2,128,2048]{2,1,0:T(8,128)(2,1)S(1)} %get-tuple-element.179.refs_0_, bf16[2,128,2048]{2,1,0:T(8,128)(2,1)S(1)} %collective-permute-done.refs_1_, bf16[2,128,2048]{2,1,0:T(8,128)(2,1)S(1)} %collective-permute-done.2.refs_0_.refs_2_, ...), custom_call_target="tpu_custom_call" | custom-call | flops 1 | bytes 1 | tf_op jit(solution)/shard_map/in_blocks/pallas_call | solution.py:124
  64.6 5.8 %collective-permute-done.11 = bf16[2,128,2048]{2,1,0:T(8,128)(2,1)S(1)} collective-permute-done((bf16[2,128,2048]{2,1,0:T(8,128)(2,1)S(1)}, bf16[2,128,2048]{2,1,0:T(8,128)(2,1)S(1)}, u32[]{:S(2)}, u32[]{:S(2)}) %collective-permute-start.11) | collective-permute-done | bytes 1048608 | tf_op jit(solution)/shard_map/ppermute | solution.py:39
  71.8 3.5 %out_blocks.3.later_ref = bf16[4,512,512]{2,1,0:T(8,128)(2,1)S(1)} custom-call(s32[2]{0:T(128)S(1)} %get-tuple-element.151.me_ref, bf16[256,1024]{1,0:T(8,128)(2,1)S(1)} %get-tuple-element.192.hidden_ref.refs_0_, bf16[256,1024]{1,0:T(8,128)(2,1)S(1)} %get-tuple-element.193.hidden_ref.refs_1_, bf16[256,1024]{1,0:T(8,128)(2,1)S(1)} %get-tuple-element.194.hidden_ref.refs_2_, ...), custom_call_target="tpu_custom_call" | custom-call | flops 1 | bytes 1 | tf_op jit(solution)/shard_map/out_blocks/pallas_call | solution.py:124
  75.3 5.7 %collective-permute-done.13.b1 = bf16[2,256,1024]{2,1,0:T(8,128)(2,1)S(1)} collective-permute-done((bf16[2,256,1024]{2,1,0:T(8,128)(2,1)S(1)}, bf16[2,256,1024]{2,1,0:T(8,128)(2,1)S(1)}, u32[]{:S(2)}, u32[]{:S(2)}) %collective-permute-start.13) | collective-permute-done | bytes 1048608 | tf_op jit(solution)/shard_map/ppermute | solution.py:29
  86.5 2.4 %collective-permute-start.17 = (bf16[256,1024]{1,0:T(8,128)(2,1)S(1)}, bf16[256,1024]{1,0:T(8,128)(2,1)S(1)}, u32[]{:S(2)}, u32[]{:S(2)}) collective-permute-start(bf16[256,1024]{1,0:T(8,128)(2,1)S(1)} %get-tuple-element.236), channel_id=1, source_target_pairs={{0,32},{8,40},{16,48},{24,56},{32,64},{40,72},{48,80},{56,88},{64,... | collective-permute-start | bytes 1572872 | tf_op jit(solution)/shard_map/ppermute | solution.py:29
  89.2 3.0 %collective-permute-start.20 = (bf16[512,512]{1,0:T(8,128)(2,1)S(1)}, bf16[512,512]{1,0:T(8,128)(2,1)S(1)}, u32[]{:S(2)}, u32[]{:S(2)}) collective-permute-start(bf16[512,512]{1,0:T(8,128)(2,1)S(1)} %get-tuple-element.233), channel_id=1, source_target_pairs={{0,24},{8,0},{16,8},{24,16},{32,56},{40,32},{48,40},{56,48},{64,88... | collective-permute-start | bytes 1572872 | tf_op jit(solution)/shard_map/ppermute | solution.py:34
  92.2 8.5 %collective-permute-done.18.a1 = bf16[256,1024]{1,0:T(8,128)(2,1)S(1)} collective-permute-done((bf16[256,1024]{1,0:T(8,128)(2,1)S(1)}, bf16[256,1024]{1,0:T(8,128)(2,1)S(1)}, u32[]{:S(2)}, u32[]{:S(2)}) %collective-permute-start.18) | collective-permute-done | bytes 524320 | tf_op jit(solution)/shard_map/ppermute | solution.py:29
  103.1 3.4 %collective-permute-done.19.b0 = bf16[512,512]{1,0:T(8,128)(2,1)S(1)} collective-permute-done((bf16[512,512]{1,0:T(8,128)(2,1)S(1)}, bf16[512,512]{1,0:T(8,128)(2,1)S(1)}, u32[]{:S(2)}, u32[]{:S(2)}) %collective-permute-start.19) | collective-permute-done | bytes 524320 | tf_op jit(solution)/shard_map/ppermute | solution.py:34
  121.6 2.9 %collective-permute-done.23.refs_2_ = bf16[128,1024]{1,0:T(8,128)(2,1)S(1)} collective-permute-done((bf16[128,1024]{1,0:T(8,128)(2,1)S(1)}, bf16[128,1024]{1,0:T(8,128)(2,1)S(1)}, u32[]{:S(2)}, u32[]{:S(2)}) %collective-permute-start.23) | collective-permute-done | bytes 262176 | tf_op jit(solution)/shard_map/ppermute | solution.py:34
  125.7 2.4 %collective-permute-done.27.refs_7_ = bf16[1024,128]{1,0:T(8,128)(2,1)S(1)} collective-permute-done((bf16[1024,128]{1,0:T(8,128)(2,1)S(1)}, bf16[1024,128]{1,0:T(8,128)(2,1)S(1)}, u32[]{:S(2)}, u32[]{:S(2)}) %collective-permute-start.27) | collective-permute-done | bytes 262176 | tf_op jit(solution)/shard_map/ppermute | solution.py:29
  (65 shorter events, 43.5 us)
Async XLA Ops:
  3.8 14.9 %collective-permute-start.2 = (bf16[2,128,2048]{2,1,0:T(8,128)(2,1)S(1)}, bf16[2,128,2048]{2,1,0:T(8,128)(2,1)S(1)}, u32[]{:S(2)}, u32[]{:S(2)}) collective-permute-start(bf16[2,128,2048]{2,1,0:T(8,128)(2,1)S(1)} %get-tuple-element.179.refs_0_), channel_id=1, source_target_pairs={{0,2},{1,7},{2,4},{3,1},{4,6},{5,3},{6,0},{7,5},{8,10},{9,15},{10,... | collective-permute-start | bytes 3145736 | tf_op jit(solution)/shard_map/ppermute | solution.py:39
  6.4 23.5 %collective-permute-start.1 = (bf16[2,128,2048]{2,1,0:T(8,128)(2,1)S(1)}, bf16[2,128,2048]{2,1,0:T(8,128)(2,1)S(1)}, u32[]{:S(2)}, u32[]{:S(2)}) collective-permute-start(bf16[2,128,2048]{2,1,0:T(8,128)(2,1)S(1)} %collective-permute-done.refs_1_), channel_id=1, source_target_pairs={{0,2},{1,7},{2,4},{3,1},{4,6},{5,3},{6,0},{7,5},{8,10},{9,15},{10,... | collective-permute-start | bytes 3145736 | tf_op jit(solution)/shard_map/ppermute | solution.py:39
  18.7 5.6 %collective-permute-start.4 = (bf16[1,128,2048]{2,1,0:T(8,128)(2,1)S(1)}, bf16[1,128,2048]{2,1,0:T(8,128)(2,1)S(1)}, u32[]{:S(2)}, u32[]{:S(2)}) collective-permute-start(bf16[1,128,2048]{2,1,0:T(8,128)(2,1)S(1)} %get-tuple-element.241), channel_id=1, source_target_pairs={{0,1},{1,0},{2,3},{3,2},{4,5},{5,4},{6,7},{7,6},{8,9},{9,8},{10,11... | collective-permute-start | bytes 1572872 | tf_op jit(solution)/shard_map/ppermute | solution.py:43
  18.8 5.5 %collective-permute-start.3 = (bf16[1,128,2048]{2,1,0:T(8,128)(2,1)S(1)}, bf16[1,128,2048]{2,1,0:T(8,128)(2,1)S(1)}, u32[]{:S(2)}, u32[]{:S(2)}) collective-permute-start(bf16[1,128,2048]{2,1,0:T(8,128)(2,1)S(1)} %get-tuple-element.242), channel_id=1, source_target_pairs={{0,1},{1,0},{2,3},{3,2},{4,5},{5,4},{6,7},{7,6},{8,9},{9,8},{10,11... | collective-permute-start | bytes 1572872 | tf_op jit(solution)/shard_map/ppermute | solution.py:43
  22.2 11.2 %collective-permute-start.7 = (bf16[1,2,128,2048]{3,2,1,0:T(8,128)(2,1)S(1)}, bf16[1,2,128,2048]{3,2,1,0:T(8,128)(2,1)S(1)}, u32[]{:S(2)}, u32[]{:S(2)}) collective-permute-start(bf16[1,2,128,2048]{3,2,1,0:T(8,128)(2,1)S(1)} %get-tuple-element.129), channel_id=1, source_target_pairs={{0,1},{1,0},{2,3},{3,2},{4,5},{5,4},{6,7},{7,6},{8,9},{9,8},{10,11... | collective-permute-start | bytes 3145736 | tf_op jit(solution)/shard_map/ppermute | solution.py:43
  22.4 18.7 %collective-permute-start.8 = (bf16[2,128,2048]{2,1,0:T(8,128)(2,1)S(1)}, bf16[2,128,2048]{2,1,0:T(8,128)(2,1)S(1)}, u32[]{:S(2)}, u32[]{:S(2)}) collective-permute-start(bf16[2,128,2048]{2,1,0:T(8,128)(2,1)S(1)} %collective-permute-done.2.refs_0_.refs_2_), channel_id=1, source_target_pairs={{0,2},{1,7},{2,4},{3,1},{4,6},{5,3},{6,0},{7,5},{8,10},{9,15},{10,... | collective-permute-start | bytes 3145736 | tf_op jit(solution)/shard_map/ppermute | solution.py:39
  30.0 3.5 %collective-permute-start.6 = (bf16[1,128,2048]{2,1,0:T(8,128)(2,1)S(1)}, bf16[1,128,2048]{2,1,0:T(8,128)(2,1)S(1)}, u32[]{:S(2)}, u32[]{:S(2)}) collective-permute-start(bf16[1,128,2048]{2,1,0:T(8,128)(2,1)S(1)} %get-tuple-element.239), channel_id=1, source_target_pairs={{0,1},{1,0},{2,3},{3,2},{4,5},{5,4},{6,7},{7,6},{8,9},{9,8},{10,11... | collective-permute-start | bytes 1572872 | tf_op jit(solution)/shard_map/ppermute | solution.py:43
  49.0 6.1 %collective-permute-start.10 = (bf16[3,2,128,2048]{3,2,1,0:T(8,128)(2,1)S(1)}, bf16[3,2,128,2048]{3,2,1,0:T(8,128)(2,1)S(1)}, u32[]{:S(2)}, u32[]{:S(2)}) collective-permute-start(bf16[3,2,128,2048]{3,2,1,0:T(8,128)(2,1)S(1)} %get-tuple-element.150), channel_id=1, source_target_pairs={{0,1},{1,0},{2,3},{3,2},{4,5},{5,4},{6,7},{7,6},{8,9},{9,8},{10,11... | collective-permute-start | bytes 9437192 | tf_op jit(solution)/shard_map/ppermute | solution.py:43
  55.5 14.9 %collective-permute-start.11 = (bf16[2,128,2048]{2,1,0:T(8,128)(2,1)S(1)}, bf16[2,128,2048]{2,1,0:T(8,128)(2,1)S(1)}, u32[]{:S(2)}, u32[]{:S(2)}) collective-permute-start(bf16[2,128,2048]{2,1,0:T(8,128)(2,1)S(1)} %fusion.3), channel_id=1, source_target_pairs={{0,6},{1,3},{2,0},{3,5},{4,2},{5,7},{6,4},{7,1},{8,14},{9,11},{10,... | collective-permute-start | bytes 3145736 | tf_op jit(solution)/shard_map/ppermute | solution.py:39
  55.7 25.3 %collective-permute-start.13 = (bf16[2,256,1024]{2,1,0:T(8,128)(2,1)S(1)}, bf16[2,256,1024]{2,1,0:T(8,128)(2,1)S(1)}, u32[]{:S(2)}, u32[]{:S(2)}) collective-permute-start(bf16[2,256,1024]{2,1,0:T(8,128)(2,1)S(1)} %get-tuple-element.166), channel_id=1, source_target_pairs={{0,32},{8,40},{16,48},{24,56},{32,64},{40,72},{48,80},{56,88},{64,... | collective-permute-start | bytes 3145736 | tf_op jit(solution)/shard_map/ppermute | solution.py:29
  56.2 26.8 %collective-permute-start.14 = (bf16[2,256,1024]{2,1,0:T(8,128)(2,1)S(1)}, bf16[2,256,1024]{2,1,0:T(8,128)(2,1)S(1)}, u32[]{:S(2)}, u32[]{:S(2)}) collective-permute-start(bf16[2,256,1024]{2,1,0:T(8,128)(2,1)S(1)} %get-tuple-element.167), channel_id=1, source_target_pairs={{0,96},{8,104},{16,112},{24,120},{32,0},{40,8},{48,16},{56,24},{64... | collective-permute-start | bytes 3145736 | tf_op jit(solution)/shard_map/ppermute | solution.py:29
  57.7 27.0 %collective-permute-start.15 = (bf16[2,512,512]{2,1,0:T(8,128)(2,1)S(1)}, bf16[2,512,512]{2,1,0:T(8,128)(2,1)S(1)}, u32[]{:S(2)}, u32[]{:S(2)}) collective-permute-start(bf16[2,512,512]{2,1,0:T(8,128)(2,1)S(1)} %get-tuple-element.176), channel_id=1, source_target_pairs={{0,8},{8,16},{16,24},{24,0},{32,40},{40,48},{48,56},{56,32},{64,72... | collective-permute-start | bytes 3145736 | tf_op jit(solution)/shard_map/ppermute | solution.py:34
  59.3 26.0 %collective-permute-start.16 = (bf16[2,512,512]{2,1,0:T(8,128)(2,1)S(1)}, bf16[2,512,512]{2,1,0:T(8,128)(2,1)S(1)}, u32[]{:S(2)}, u32[]{:S(2)}) collective-permute-start(bf16[2,512,512]{2,1,0:T(8,128)(2,1)S(1)} %get-tuple-element.177), channel_id=1, source_target_pairs={{0,24},{8,0},{16,8},{24,16},{32,56},{40,32},{48,40},{56,48},{64,88... | collective-permute-start | bytes 3145736 | tf_op jit(solution)/shard_map/ppermute | solution.py:34
  71.4 35.1 %collective-permute-start.12 = (bf16[2,2,128,2048]{3,2,1,0:T(8,128)(2,1)S(1)}, bf16[2,2,128,2048]{3,2,1,0:T(8,128)(2,1)S(1)}, u32[]{:S(2)}, u32[]{:S(2)}) collective-permute-start(bf16[2,2,128,2048]{3,2,1,0:T(8,128)(2,1)S(1)} %add_convert_fusion), channel_id=1, source_target_pairs={{0,6},{1,3},{2,0},{3,5},{4,2},{5,7},{6,4},{7,1},{8,14},{9,11},{10,... | collective-permute-start | bytes 6291464 | tf_op jit(solution)/shard_map/ppermute | solution.py:39
  85.6 15.1 %collective-permute-start.18 = (bf16[256,1024]{1,0:T(8,128)(2,1)S(1)}, bf16[256,1024]{1,0:T(8,128)(2,1)S(1)}, u32[]{:S(2)}, u32[]{:S(2)}) collective-permute-start(bf16[256,1024]{1,0:T(8,128)(2,1)S(1)} %get-tuple-element.235), channel_id=1, source_target_pairs={{0,96},{8,104},{16,112},{24,120},{32,0},{40,8},{48,16},{56,24},{64... | collective-permute-start | bytes 1572872 | tf_op jit(solution)/shard_map/ppermute | solution.py:29
  86.5 14.3 %collective-permute-start.17 = (bf16[256,1024]{1,0:T(8,128)(2,1)S(1)}, bf16[256,1024]{1,0:T(8,128)(2,1)S(1)}, u32[]{:S(2)}, u32[]{:S(2)}) collective-permute-start(bf16[256,1024]{1,0:T(8,128)(2,1)S(1)} %get-tuple-element.236), channel_id=1, source_target_pairs={{0,32},{8,40},{16,48},{24,56},{32,64},{40,72},{48,80},{56,88},{64,... | collective-permute-start | bytes 1572872 | tf_op jit(solution)/shard_map/ppermute | solution.py:29
  89.2 13.8 %collective-permute-start.20 = (bf16[512,512]{1,0:T(8,128)(2,1)S(1)}, bf16[512,512]{1,0:T(8,128)(2,1)S(1)}, u32[]{:S(2)}, u32[]{:S(2)}) collective-permute-start(bf16[512,512]{1,0:T(8,128)(2,1)S(1)} %get-tuple-element.233), channel_id=1, source_target_pairs={{0,24},{8,0},{16,8},{24,16},{32,56},{40,32},{48,40},{56,48},{64,88... | collective-permute-start | bytes 1572872 | tf_op jit(solution)/shard_map/ppermute | solution.py:34
  92.2 14.3 %collective-permute-start.19 = (bf16[512,512]{1,0:T(8,128)(2,1)S(1)}, bf16[512,512]{1,0:T(8,128)(2,1)S(1)}, u32[]{:S(2)}, u32[]{:S(2)}) collective-permute-start(bf16[512,512]{1,0:T(8,128)(2,1)S(1)} %get-tuple-element.234), channel_id=1, source_target_pairs={{0,8},{8,16},{16,24},{24,0},{32,40},{40,48},{48,56},{56,32},{64,72... | collective-permute-start | bytes 1572872 | tf_op jit(solution)/shard_map/ppermute | solution.py:34
  109.3 10.7 %collective-permute-start.22 = (bf16[128,1024]{1,0:T(8,128)(2,1)S(1)}, bf16[128,1024]{1,0:T(8,128)(2,1)S(1)}, u32[]{:S(2)}, u32[]{:S(2)}) collective-permute-start(bf16[128,1024]{1,0:T(8,128)(2,1)S(1)} %get-tuple-element.216), channel_id=1, source_target_pairs={{0,16},{8,24},{16,0},{24,8},{32,48},{40,56},{48,32},{56,40},{64,80... | collective-permute-start | bytes 786440 | tf_op jit(solution)/shard_map/ppermute | solution.py:34
  109.3 15.2 %collective-permute-start.23 = (bf16[128,1024]{1,0:T(8,128)(2,1)S(1)}, bf16[128,1024]{1,0:T(8,128)(2,1)S(1)}, u32[]{:S(2)}, u32[]{:S(2)}) collective-permute-start(bf16[128,1024]{1,0:T(8,128)(2,1)S(1)} %get-tuple-element.217), channel_id=1, source_target_pairs={{0,8},{8,16},{16,24},{24,0},{32,40},{40,48},{48,56},{56,32},{64,72... | collective-permute-start | bytes 786440 | tf_op jit(solution)/shard_map/ppermute | solution.py:34
  110.5 14.0 %collective-permute-start.24 = (bf16[128,1024]{1,0:T(8,128)(2,1)S(1)}, bf16[128,1024]{1,0:T(8,128)(2,1)S(1)}, u32[]{:S(2)}, u32[]{:S(2)}) collective-permute-start(bf16[128,1024]{1,0:T(8,128)(2,1)S(1)} %get-tuple-element.218), channel_id=1, source_target_pairs={{0,24},{8,0},{16,8},{24,16},{32,56},{40,32},{48,40},{56,48},{64,88... | collective-permute-start | bytes 786440 | tf_op jit(solution)/shard_map/ppermute | solution.py:34
  112.6 11.9 %collective-permute-start.25 = (bf16[1024,128]{1,0:T(8,128)(2,1)S(1)}, bf16[1024,128]{1,0:T(8,128)(2,1)S(1)}, u32[]{:S(2)}, u32[]{:S(2)}) collective-permute-start(bf16[1024,128]{1,0:T(8,128)(2,1)S(1)} %get-tuple-element.220), channel_id=1, source_target_pairs={{0,64},{8,72},{16,80},{24,88},{32,96},{40,104},{48,112},{56,120},{... | collective-permute-start | bytes 786440 | tf_op jit(solution)/shard_map/ppermute | solution.py:29
  112.8 12.9 %collective-permute-start.26 = (bf16[1024,128]{1,0:T(8,128)(2,1)S(1)}, bf16[1024,128]{1,0:T(8,128)(2,1)S(1)}, u32[]{:S(2)}, u32[]{:S(2)}) collective-permute-start(bf16[1024,128]{1,0:T(8,128)(2,1)S(1)} %get-tuple-element.221), channel_id=1, source_target_pairs={{0,32},{8,40},{16,48},{24,56},{32,64},{40,72},{48,80},{56,88},{64,... | collective-permute-start | bytes 786440 | tf_op jit(solution)/shard_map/ppermute | solution.py:29
  120.0 8.1 %collective-permute-start.27 = (bf16[1024,128]{1,0:T(8,128)(2,1)S(1)}, bf16[1024,128]{1,0:T(8,128)(2,1)S(1)}, u32[]{:S(2)}, u32[]{:S(2)}) collective-permute-start(bf16[1024,128]{1,0:T(8,128)(2,1)S(1)} %get-tuple-element.222), channel_id=1, source_target_pairs={{0,96},{8,104},{16,112},{24,120},{32,0},{40,8},{48,16},{56,24},{64... | collective-permute-start | bytes 786440 | tf_op jit(solution)/shard_map/ppermute | solution.py:29
  (7 other events, 26.7 us)

commit v3 on v2

--- a/solution.py
+++ b/solution.py
@@ -390,7 +390,7 @@
     near_other = after(near_other, near)
     swapped_other = [swap_core(near_other[:1]), swap_core(near_other[1:])]
     swapped_other, own_got = after((swapped_other, own_got), near_terms)
-    other = hidden_units([[near_other], swapped_other], w_in, w_out)
+    other = hidden_units([[near_other], swapped_other], w_in, w_out, True)
     near_terms = row_terms(other[0], other[1], w_in, w_out, routed, 3, 1, near_terms)
 
     far_mine = after(far_mine, near_terms)

time: 129 us -> 129 us (level)
  transfers between devices with their start and end apart: 28 -> 28, of which waited for: 18 -> 18; matrix products, arithmetic and copies ran while one was open for 5% -> 5% of each run, Pallas kernels for 30% -> 29%
where the time goes in v3:
time: 129 us
  waiting for transfers between devices  49.8 us (39%)
  Pallas kernels  46.4 us (36%)
  starting transfers between devices  24.7 us (19%)
  other arithmetic  4.29 us (3%)
  matrix products  2.14 us (2%)
  between operations  1.56 us (1%)
    pallas_call x12, Pallas kernels, on_held(): pl.pallas_call(body, in_specs=[IN_SMEM] * len(first) + [IN_VMEM] * len(ar...  37.2 us
    ppermute x7, waiting for transfers between devices, move_x(): return lax.ppermute(v, 'ctx', perm)  19.8 us
    ppermute x5, waiting for transfers between devices, move_lane(): return lax.ppermute(v, 'head', perm)  12.7 us
    ppermute x7, waiting for transfers between devices, move_y(): return lax.ppermute(v, 'ctx', perm)  12.2 us
    ppermute x7, starting transfers between devices, move_y(): return lax.ppermute(v, 'ctx', perm)  9.46 us
    ppermute x7, starting transfers between devices, move_x(): return lax.ppermute(v, 'ctx', perm)  7.62 us
    ppermute x5, starting transfers between devices, move_lane(): return lax.ppermute(v, 'head', perm)  5.95 us
    ppermute x9, waiting for transfers between devices, swap_core(): return lax.ppermute(v, 'head', [(i, i ^ 1) for i in range(2 * SIDE)])  5.08 us
  transfers between devices with their start and end apart: 28, of which 18 were waited for; matrix products, arithmetic and copies ran while one was open for 5% of the time, Pallas kernels for 29%

profile of v3, /device:TPU:70, one launch (start us, length us, event | category | flops | bytes accessed | tf_op | source)
XLA Modules:
  0.0 129.2 jit_solution(9414889109161144202)
XLA Ops:
  1.3 2.4 %take_rows.1 = (bf16[2,128,2048]{2,1,0:T(8,128)(2,1)S(1)}, s32[2]{0:T(128)S(1)}) custom-call(s32[1]{0:T(128)S(6)} %copy.20.counts_ref, s32[1,128]{1,0:T(1,128)} %bitcast.31, f32[1,128]{1,0:T(1,128)} %bitcast.30, bf16[512,2048]{1,0:T(8,128)(2,1)} %tokens_ref.1, bf16[128,2048]{1,0:T(8,128)(2,1)} %cotan_ref.1), custom_call_target="tpu_custom_call" | custom-call | flops 1 | bytes 1 | tf_op jit(solution)/shard_map/take_rows/pallas_call | solution.py:97
  8.0 3.5 %hold_weights.1 = (bf16[2048,1024]{1,0:T(8,128)(2,1)S(1)}, bf16[1024,2048]{1,0:T(8,128)(2,1)S(1)}) custom-call(bf16[2048,1024]{1,0:T(8,128)(2,1)} %win_ref, bf16[1024,2048]{1,0:T(8,128)(2,1)} %wout_ref), custom_call_target="tpu_custom_call" | custom-call | flops 1 | bytes 1 | tf_op jit(solution)/shard_map/hold_weights/pallas_call | solution.py:198
  11.5 3.8 %hidden_units.4 = (bf16[256,1024]{1,0:T(8,128)(2,1)S(1)}, bf16[256,1024]{1,0:T(8,128)(2,1)S(1)}, bf16[256,2048]{1,0:T(8,128)(2,1)S(1)}) custom-call(bf16[2,128,2048]{2,1,0:T(8,128)(2,1)S(1)} %get-tuple-element.179.refs_0_, bf16[2,128,2048]{2,1,0:T(8,128)(2,1)S(1)} %collective-permute-done.refs_1_, ...), custom_call_target="tpu_custom_call" | custom-call | flops 1 | bytes 1 | tf_op jit(solution)/shard_map/hidden_units/pallas_call | solution.py:124
  15.3 3.3 %collective-permute-done.2.refs_0_.refs_2_ = bf16[2,128,2048]{2,1,0:T(8,128)(2,1)S(1)} collective-permute-done((bf16[2,128,2048]{2,1,0:T(8,128)(2,1)S(1)}, bf16[2,128,2048]{2,1,0:T(8,128)(2,1)S(1)}, u32[]{:S(2)}, u32[]{:S(2)}) %collective-permute-start.2) | collective-permute-done | bytes 1048608 | tf_op jit(solution)/shard_map/ppermute | solution.py:39
  19.3 2.8 %row_terms.4 = (bf16[1,2,128,2048]{3,2,1,0:T(8,128)(2,1)S(1)}, bf16[1,2,128,2048]{3,2,1,0:T(8,128)(2,1)S(1)}) custom-call(bf16[256,1024]{1,0:T(8,128)(2,1)S(1)} %get-tuple-element.192.hidden_ref.refs_0_, bf16[256,1024]{1,0:T(8,128)(2,1)S(1)} %get-tuple-element.187.dpre_ref.refs_8_, bf16[2048,1024]{1,0:T(8,128)(2,1)S(1)} %get-tuple-element.122.refs_2_.win_ref.refs_3_, ...), custom_call_target="tpu_custom_call" | custom-call | flops 1 | bytes 1 | tf_op jit(solution)/shard_map/row_terms/pallas_call | solution.py:124
  24.4 3.8 %hidden_units.5 = (bf16[256,1024]{1,0:T(8,128)(2,1)S(1)}, bf16[256,1024]{1,0:T(8,128)(2,1)S(1)}, bf16[256,2048]{1,0:T(8,128)(2,1)S(1)}) custom-call(bf16[2,128,2048]{2,1,0:T(8,128)(2,1)S(1)} %collective-permute-done.2.refs_0_.refs_2_, bf16[1,128,2048]{2,1,0:T(8,128)(2,1)S(1)} %collective-permute-done.3.refs_1_.refs_3_, ...), custom_call_target="tpu_custom_call" | custom-call | flops 1 | bytes 1 | tf_op jit(solution)/shard_map/hidden_units/pallas_call | solution.py:124
  30.6 2.8 %row_terms.5 = (bf16[3,2,128,2048]{3,2,1,0:T(8,128)(2,1)S(1)}, bf16[3,2,128,2048]{3,2,1,0:T(8,128)(2,1)S(1)}) custom-call(bf16[256,1024]{1,0:T(8,128)(2,1)S(1)} %get-tuple-element.193.hidden_ref.refs_1_, bf16[256,1024]{1,0:T(8,128)(2,1)S(1)} %get-tuple-element.188.dpre_ref.refs_9_, bf16[2048,1024]{1,0:T(8,128)(2,1)S(1)} %get-tuple-element.122.refs_2_.win_ref.refs_3_, ...), custom_call_target="tpu_custom_call" | custom-call | flops 1 | bytes 1 | tf_op jit(solution)/shard_map/row_terms/pallas_call | solution.py:124
  33.5 2.9 %hidden_units.6 = (bf16[256,1024]{1,0:T(8,128)(2,1)S(1)}, bf16[256,1024]{1,0:T(8,128)(2,1)S(1)}, bf16[256,2048]{1,0:T(8,128)(2,1)S(1)}) custom-call(bf16[2,128,2048]{2,1,0:T(8,128)(2,1)S(1)} %collective-permute-done.1.refs_0_.refs_4_, bf16[1,128,2048]{2,1,0:T(8,128)(2,1)S(1)} %collective-permute-done.5.refs_1_.refs_5_, ...), custom_call_target="tpu_custom_call" | custom-call | flops 1 | bytes 1 | tf_op jit(solution)/shard_map/hidden_units/pallas_call | solution.py:124
  36.3 2.9 %row_terms.6 = (bf16[3,2,128,2048]{3,2,1,0:T(8,128)(2,1)S(1)}, bf16[3,2,128,2048]{3,2,1,0:T(8,128)(2,1)S(1)}) custom-call(bf16[256,1024]{1,0:T(8,128)(2,1)S(1)} %get-tuple-element.194.hidden_ref.refs_2_, bf16[256,1024]{1,0:T(8,128)(2,1)S(1)} %get-tuple-element.189.dpre_ref.refs_10_, ...), custom_call_target="tpu_custom_call", output_to_operand_aliasing={{0}: (4, {}), {1}: (5, {})} | custom-call | flops 1 | bytes 1 | tf_op jit(solution)/shard_map/row_terms/pallas_call | solution.py:124
  41.1 2.7 %collective-permute-done.9.refs_1_.refs_7_ = bf16[2,128,2048]{2,1,0:T(8,128)(2,1)S(1)} collective-permute-done((bf16[2,128,2048]{2,1,0:T(8,128)(2,1)S(1)}, bf16[2,128,2048]{2,1,0:T(8,128)(2,1)S(1)}, u32[]{:S(2)}, u32[]{:S(2)}) %collective-permute-start.9) | collective-permute-done | bytes 1048608 | tf_op jit(solution)/shard_map/ppermute | solution.py:43
  43.8 2.9 %hidden_units.7 = (bf16[256,1024]{1,0:T(8,128)(2,1)S(1)}, bf16[256,1024]{1,0:T(8,128)(2,1)S(1)}, bf16[256,2048]{1,0:T(8,128)(2,1)S(1)}) custom-call(bf16[2,128,2048]{2,1,0:T(8,128)(2,1)S(1)} %collective-permute-done.8.refs_0_.refs_6_, bf16[2,128,2048]{2,1,0:T(8,128)(2,1)S(1)} %collective-permute-done.9.refs_1_.refs_7_, ...), custom_call_target="tpu_custom_call" | custom-call | flops 1 | bytes 1 | tf_op jit(solution)/shard_map/hidden_units/pallas_call | solution.py:124
  46.6 2.4 %row_terms.7 = (bf16[3,2,128,2048]{3,2,1,0:T(8,128)(2,1)S(1)}, bf16[3,2,128,2048]{3,2,1,0:T(8,128)(2,1)S(1)}) custom-call(bf16[256,1024]{1,0:T(8,128)(2,1)S(1)} %get-tuple-element.195.hidden_ref.refs_3_, bf16[256,1024]{1,0:T(8,128)(2,1)S(1)} %get-tuple-element.190.dpre_ref.refs_11_, ...), custom_call_target="tpu_custom_call", output_to_operand_aliasing={{0}: (4, {}), {1}: (5, {})} | custom-call | flops 1 | bytes 1 | tf_op jit(solution)/shard_map/row_terms/pallas_call | solution.py:124
  49.2 2.9 %in_blocks.2 = (bf16[2,256,1024]{2,1,0:T(8,128)(2,1)S(1)}, bf16[2,256,1024]{2,1,0:T(8,128)(2,1)S(1)}) custom-call(s32[2]{0:T(128)S(1)} %get-tuple-element.151.me_ref, bf16[2,128,2048]{2,1,0:T(8,128)(2,1)S(1)} %get-tuple-element.179.refs_0_, bf16[2,128,2048]{2,1,0:T(8,128)(2,1)S(1)} %collective-permute-done.refs_1_, ...), custom_call_target="tpu_custom_call" | custom-call | flops 1 | bytes 1 | tf_op jit(solution)/shard_map/in_blocks/pallas_call | solution.py:124
  52.2 2.9 %out_blocks.2 = (bf16[2,512,512]{2,1,0:T(8,128)(2,1)S(1)}, bf16[2,512,512]{2,1,0:T(8,128)(2,1)S(1)}) custom-call(s32[2]{0:T(128)S(1)} %get-tuple-element.151.me_ref, bf16[256,1024]{1,0:T(8,128)(2,1)S(1)} %get-tuple-element.192.hidden_ref.refs_0_, bf16[256,1024]{1,0:T(8,128)(2,1)S(1)} %get-tuple-element.193.hidden_ref.refs_1_, ...), custom_call_target="tpu_custom_call" | custom-call | flops 1 | bytes 1 | tf_op jit(solution)/shard_map/out_blocks/pallas_call | solution.py:124
  61.0 3.6 %in_blocks.3.later_ref = bf16[4,256,1024]{2,1,0:T(8,128)(2,1)S(1)} custom-call(s32[2]{0:T(128)S(1)} %get-tuple-element.151.me_ref, bf16[2,128,2048]{2,1,0:T(8,128)(2,1)S(1)} %get-tuple-element.179.refs_0_, bf16[2,128,2048]{2,1,0:T(8,128)(2,1)S(1)} %collective-permute-done.refs_1_, bf16[2,128,2048]{2,1,0:T(8,128)(2,1)S(1)} %collective-permute-done.2.refs_0_.refs_2_, ...), custom_call_target="tpu_custom_call" | custom-call | flops 1 | bytes 1 | tf_op jit(solution)/shard_map/in_blocks/pallas_call | solution.py:124
  64.6 5.8 %collective-permute-done.11 = bf16[2,128,2048]{2,1,0:T(8,128)(2,1)S(1)} collective-permute-done((bf16[2,128,2048]{2,1,0:T(8,128)(2,1)S(1)}, bf16[2,128,2048]{2,1,0:T(8,128)(2,1)S(1)}, u32[]{:S(2)}, u32[]{:S(2)}) %collective-permute-start.11) | collective-permute-done | bytes 1048608 | tf_op jit(solution)/shard_map/ppermute | solution.py:39
  71.8 3.5 %out_blocks.3.later_ref = bf16[4,512,512]{2,1,0:T(8,128)(2,1)S(1)} custom-call(s32[2]{0:T(128)S(1)} %get-tuple-element.151.me_ref, bf16[256,1024]{1,0:T(8,128)(2,1)S(1)} %get-tuple-element.192.hidden_ref.refs_0_, bf16[256,1024]{1,0:T(8,128)(2,1)S(1)} %get-tuple-element.193.hidden_ref.refs_1_, bf16[256,1024]{1,0:T(8,128)(2,1)S(1)} %get-tuple-element.194.hidden_ref.refs_2_, ...), custom_call_target="tpu_custom_call" | custom-call | flops 1 | bytes 1 | tf_op jit(solution)/shard_map/out_blocks/pallas_call | solution.py:124
  75.3 5.7 %collective-permute-done.13.b1 = bf16[2,256,1024]{2,1,0:T(8,128)(2,1)S(1)} collective-permute-done((bf16[2,256,1024]{2,1,0:T(8,128)(2,1)S(1)}, bf16[2,256,1024]{2,1,0:T(8,128)(2,1)S(1)}, u32[]{:S(2)}, u32[]{:S(2)}) %collective-permute-start.13) | collective-permute-done | bytes 1048608 | tf_op jit(solution)/shard_map/ppermute | solution.py:29
  86.5 2.4 %collective-permute-start.17 = (bf16[256,1024]{1,0:T(8,128)(2,1)S(1)}, bf16[256,1024]{1,0:T(8,128)(2,1)S(1)}, u32[]{:S(2)}, u32[]{:S(2)}) collective-permute-start(bf16[256,1024]{1,0:T(8,128)(2,1)S(1)} %get-tuple-element.236), channel_id=1, source_target_pairs={{0,32},{8,40},{16,48},{24,56},{32,64},{40,72},{48,80},{56,88},{64,... | collective-permute-start | bytes 1572872 | tf_op jit(solution)/shard_map/ppermute | solution.py:29
  89.2 3.0 %collective-permute-start.20 = (bf16[512,512]{1,0:T(8,128)(2,1)S(1)}, bf16[512,512]{1,0:T(8,128)(2,1)S(1)}, u32[]{:S(2)}, u32[]{:S(2)}) collective-permute-start(bf16[512,512]{1,0:T(8,128)(2,1)S(1)} %get-tuple-element.233), channel_id=1, source_target_pairs={{0,24},{8,0},{16,8},{24,16},{32,56},{40,32},{48,40},{56,48},{64,88... | collective-permute-start | bytes 1572872 | tf_op jit(solution)/shard_map/ppermute | solution.py:34
  92.2 8.5 %collective-permute-done.18.a1 = bf16[256,1024]{1,0:T(8,128)(2,1)S(1)} collective-permute-done((bf16[256,1024]{1,0:T(8,128)(2,1)S(1)}, bf16[256,1024]{1,0:T(8,128)(2,1)S(1)}, u32[]{:S(2)}, u32[]{:S(2)}) %collective-permute-start.18) | collective-permute-done | bytes 524320 | tf_op jit(solution)/shard_map/ppermute | solution.py:29
  103.1 3.4 %collective-permute-done.19.b0 = bf16[512,512]{1,0:T(8,128)(2,1)S(1)} collective-permute-done((bf16[512,512]{1,0:T(8,128)(2,1)S(1)}, bf16[512,512]{1,0:T(8,128)(2,1)S(1)}, u32[]{:S(2)}, u32[]{:S(2)}) %collective-permute-start.19) | collective-permute-done | bytes 524320 | tf_op jit(solution)/shard_map/ppermute | solution.py:34
  121.6 2.9 %collective-permute-done.23.refs_2_ = bf16[128,1024]{1,0:T(8,128)(2,1)S(1)} collective-permute-done((bf16[128,1024]{1,0:T(8,128)(2,1)S(1)}, bf16[128,1024]{1,0:T(8,128)(2,1)S(1)}, u32[]{:S(2)}, u32[]{:S(2)}) %collective-permute-start.23) | collective-permute-done | bytes 262176 | tf_op jit(solution)/shard_map/ppermute | solution.py:34
  125.7 2.4 %collective-permute-done.27.refs_7_ = bf16[1024,128]{1,0:T(8,128)(2,1)S(1)} collective-permute-done((bf16[1024,128]{1,0:T(8,128)(2,1)S(1)}, bf16[1024,128]{1,0:T(8,128)(2,1)S(1)}, u32[]{:S(2)}, u32[]{:S(2)}) %collective-permute-start.27) | collective-permute-done | bytes 262176 | tf_op jit(solution)/shard_map/ppermute | solution.py:29
  (65 shorter events, 44.4 us)
Async XLA Ops:
  3.8 14.9 %collective-permute-start.2 = (bf16[2,128,2048]{2,1,0:T(8,128)(2,1)S(1)}, bf16[2,128,2048]{2,1,0:T(8,128)(2,1)S(1)}, u32[]{:S(2)}, u32[]{:S(2)}) collective-permute-start(bf16[2,128,2048]{2,1,0:T(8,128)(2,1)S(1)} %get-tuple-element.179.refs_0_), channel_id=1, source_target_pairs={{0,2},{1,7},{2,4},{3,1},{4,6},{5,3},{6,0},{7,5},{8,10},{9,15},{10,... | collective-permute-start | bytes 3145736 | tf_op jit(solution)/shard_map/ppermute | solution.py:39
  6.4 23.5 %collective-permute-start.1 = (bf16[2,128,2048]{2,1,0:T(8,128)(2,1)S(1)}, bf16[2,128,2048]{2,1,0:T(8,128)(2,1)S(1)}, u32[]{:S(2)}, u32[]{:S(2)}) collective-permute-start(bf16[2,128,2048]{2,1,0:T(8,128)(2,1)S(1)} %collective-permute-done.refs_1_), channel_id=1, source_target_pairs={{0,2},{1,7},{2,4},{3,1},{4,6},{5,3},{6,0},{7,5},{8,10},{9,15},{10,... | collective-permute-start | bytes 3145736 | tf_op jit(solution)/shard_map/ppermute | solution.py:39
  18.7 5.6 %collective-permute-start.4 = (bf16[1,128,2048]{2,1,0:T(8,128)(2,1)S(1)}, bf16[1,128,2048]{2,1,0:T(8,128)(2,1)S(1)}, u32[]{:S(2)}, u32[]{:S(2)}) collective-permute-start(bf16[1,128,2048]{2,1,0:T(8,128)(2,1)S(1)} %get-tuple-element.241), channel_id=1, source_target_pairs={{0,1},{1,0},{2,3},{3,2},{4,5},{5,4},{6,7},{7,6},{8,9},{9,8},{10,11... | collective-permute-start | bytes 1572872 | tf_op jit(solution)/shard_map/ppermute | solution.py:43
  18.8 5.5 %collective-permute-start.3 = (bf16[1,128,2048]{2,1,0:T(8,128)(2,1)S(1)}, bf16[1,128,2048]{2,1,0:T(8,128)(2,1)S(1)}, u32[]{:S(2)}, u32[]{:S(2)}) collective-permute-start(bf16[1,128,2048]{2,1,0:T(8,128)(2,1)S(1)} %get-tuple-element.242), channel_id=1, source_target_pairs={{0,1},{1,0},{2,3},{3,2},{4,5},{5,4},{6,7},{7,6},{8,9},{9,8},{10,11... | collective-permute-start | bytes 1572872 | tf_op jit(solution)/shard_map/ppermute | solution.py:43
  22.2 11.2 %collective-permute-start.7 = (bf16[1,2,128,2048]{3,2,1,0:T(8,128)(2,1)S(1)}, bf16[1,2,128,2048]{3,2,1,0:T(8,128)(2,1)S(1)}, u32[]{:S(2)}, u32[]{:S(2)}) collective-permute-start(bf16[1,2,128,2048]{3,2,1,0:T(8,128)(2,1)S(1)} %get-tuple-element.129), channel_id=1, source_target_pairs={{0,1},{1,0},{2,3},{3,2},{4,5},{5,4},{6,7},{7,6},{8,9},{9,8},{10,11... | collective-permute-start | bytes 3145736 | tf_op jit(solution)/shard_map/ppermute | solution.py:43
  22.4 18.7 %collective-permute-start.8 = (bf16[2,128,2048]{2,1,0:T(8,128)(2,1)S(1)}, bf16[2,128,2048]{2,1,0:T(8,128)(2,1)S(1)}, u32[]{:S(2)}, u32[]{:S(2)}) collective-permute-start(bf16[2,128,2048]{2,1,0:T(8,128)(2,1)S(1)} %collective-permute-done.2.refs_0_.refs_2_), channel_id=1, source_target_pairs={{0,2},{1,7},{2,4},{3,1},{4,6},{5,3},{6,0},{7,5},{8,10},{9,15},{10,... | collective-permute-start | bytes 3145736 | tf_op jit(solution)/shard_map/ppermute | solution.py:39
  30.0 3.5 %collective-permute-start.6 = (bf16[1,128,2048]{2,1,0:T(8,128)(2,1)S(1)}, bf16[1,128,2048]{2,1,0:T(8,128)(2,1)S(1)}, u32[]{:S(2)}, u32[]{:S(2)}) collective-permute-start(bf16[1,128,2048]{2,1,0:T(8,128)(2,1)S(1)} %get-tuple-element.239), channel_id=1, source_target_pairs={{0,1},{1,0},{2,3},{3,2},{4,5},{5,4},{6,7},{7,6},{8,9},{9,8},{10,11... | collective-permute-start | bytes 1572872 | tf_op jit(solution)/shard_map/ppermute | solution.py:43
  49.0 6.1 %collective-permute-start.10 = (bf16[3,2,128,2048]{3,2,1,0:T(8,128)(2,1)S(1)}, bf16[3,2,128,2048]{3,2,1,0:T(8,128)(2,1)S(1)}, u32[]{:S(2)}, u32[]{:S(2)}) collective-permute-start(bf16[3,2,128,2048]{3,2,1,0:T(8,128)(2,1)S(1)} %get-tuple-element.150), channel_id=1, source_target_pairs={{0,1},{1,0},{2,3},{3,2},{4,5},{5,4},{6,7},{7,6},{8,9},{9,8},{10,11... | collective-permute-start | bytes 9437192 | tf_op jit(solution)/shard_map/ppermute | solution.py:43
  55.5 14.9 %collective-permute-start.11 = (bf16[2,128,2048]{2,1,0:T(8,128)(2,1)S(1)}, bf16[2,128,2048]{2,1,0:T(8,128)(2,1)S(1)}, u32[]{:S(2)}, u32[]{:S(2)}) collective-permute-start(bf16[2,128,2048]{2,1,0:T(8,128)(2,1)S(1)} %fusion.3), channel_id=1, source_target_pairs={{0,6},{1,3},{2,0},{3,5},{4,2},{5,7},{6,4},{7,1},{8,14},{9,11},{10,... | collective-permute-start | bytes 3145736 | tf_op jit(solution)/shard_map/ppermute | solution.py:39
  55.7 25.3 %collective-permute-start.13 = (bf16[2,256,1024]{2,1,0:T(8,128)(2,1)S(1)}, bf16[2,256,1024]{2,1,0:T(8,128)(2,1)S(1)}, u32[]{:S(2)}, u32[]{:S(2)}) collective-permute-start(bf16[2,256,1024]{2,1,0:T(8,128)(2,1)S(1)} %get-tuple-element.166), channel_id=1, source_target_pairs={{0,32},{8,40},{16,48},{24,56},{32,64},{40,72},{48,80},{56,88},{64,... | collective-permute-start | bytes 3145736 | tf_op jit(solution)/shard_map/ppermute | solution.py:29
  56.2 26.8 %collective-permute-start.14 = (bf16[2,256,1024]{2,1,0:T(8,128)(2,1)S(1)}, bf16[2,256,1024]{2,1,0:T(8,128)(2,1)S(1)}, u32[]{:S(2)}, u32[]{:S(2)}) collective-permute-start(bf16[2,256,1024]{2,1,0:T(8,128)(2,1)S(1)} %get-tuple-element.167), channel_id=1, source_target_pairs={{0,96},{8,104},{16,112},{24,120},{32,0},{40,8},{48,16},{56,24},{64... | collective-permute-start | bytes 3145736 | tf_op jit(solution)/shard_map/ppermute | solution.py:29
  57.7 27.0 %collective-permute-start.15 = (bf16[2,512,512]{2,1,0:T(8,128)(2,1)S(1)}, bf16[2,512,512]{2,1,0:T(8,128)(2,1)S(1)}, u32[]{:S(2)}, u32[]{:S(2)}) collective-permute-start(bf16[2,512,512]{2,1,0:T(8,128)(2,1)S(1)} %get-tuple-element.176), channel_id=1, source_target_pairs={{0,8},{8,16},{16,24},{24,0},{32,40},{40,48},{48,56},{56,32},{64,72... | collective-permute-start | bytes 3145736 | tf_op jit(solution)/shard_map/ppermute | solution.py:34
  59.3 26.0 %collective-permute-start.16 = (bf16[2,512,512]{2,1,0:T(8,128)(2,1)S(1)}, bf16[2,512,512]{2,1,0:T(8,128)(2,1)S(1)}, u32[]{:S(2)}, u32[]{:S(2)}) collective-permute-start(bf16[2,512,512]{2,1,0:T(8,128)(2,1)S(1)} %get-tuple-element.177), channel_id=1, source_target_pairs={{0,24},{8,0},{16,8},{24,16},{32,56},{40,32},{48,40},{56,48},{64,88... | collective-permute-start | bytes 3145736 | tf_op jit(solution)/shard_map/ppermute | solution.py:34
  71.4 35.1 %collective-permute-start.12 = (bf16[2,2,128,2048]{3,2,1,0:T(8,128)(2,1)S(1)}, bf16[2,2,128,2048]{3,2,1,0:T(8,128)(2,1)S(1)}, u32[]{:S(2)}, u32[]{:S(2)}) collective-permute-start(bf16[2,2,128,2048]{3,2,1,0:T(8,128)(2,1)S(1)} %add_convert_fusion), channel_id=1, source_target_pairs={{0,6},{1,3},{2,0},{3,5},{4,2},{5,7},{6,4},{7,1},{8,14},{9,11},{10,... | collective-permute-start | bytes 6291464 | tf_op jit(solution)/shard_map/ppermute | solution.py:39
  85.6 15.1 %collective-permute-start.18 = (bf16[256,1024]{1,0:T(8,128)(2,1)S(1)}, bf16[256,1024]{1,0:T(8,128)(2,1)S(1)}, u32[]{:S(2)}, u32[]{:S(2)}) collective-permute-start(bf16[256,1024]{1,0:T(8,128)(2,1)S(1)} %get-tuple-element.235), channel_id=1, source_target_pairs={{0,96},{8,104},{16,112},{24,120},{32,0},{40,8},{48,16},{56,24},{64... | collective-permute-start | bytes 1572872 | tf_op jit(solution)/shard_map/ppermute | solution.py:29
  86.5 14.3 %collective-permute-start.17 = (bf16[256,1024]{1,0:T(8,128)(2,1)S(1)}, bf16[256,1024]{1,0:T(8,128)(2,1)S(1)}, u32[]{:S(2)}, u32[]{:S(2)}) collective-permute-start(bf16[256,1024]{1,0:T(8,128)(2,1)S(1)} %get-tuple-element.236), channel_id=1, source_target_pairs={{0,32},{8,40},{16,48},{24,56},{32,64},{40,72},{48,80},{56,88},{64,... | collective-permute-start | bytes 1572872 | tf_op jit(solution)/shard_map/ppermute | solution.py:29
  89.2 13.8 %collective-permute-start.20 = (bf16[512,512]{1,0:T(8,128)(2,1)S(1)}, bf16[512,512]{1,0:T(8,128)(2,1)S(1)}, u32[]{:S(2)}, u32[]{:S(2)}) collective-permute-start(bf16[512,512]{1,0:T(8,128)(2,1)S(1)} %get-tuple-element.233), channel_id=1, source_target_pairs={{0,24},{8,0},{16,8},{24,16},{32,56},{40,32},{48,40},{56,48},{64,88... | collective-permute-start | bytes 1572872 | tf_op jit(solution)/shard_map/ppermute | solution.py:34
  92.2 14.3 %collective-permute-start.19 = (bf16[512,512]{1,0:T(8,128)(2,1)S(1)}, bf16[512,512]{1,0:T(8,128)(2,1)S(1)}, u32[]{:S(2)}, u32[]{:S(2)}) collective-permute-start(bf16[512,512]{1,0:T(8,128)(2,1)S(1)} %get-tuple-element.234), channel_id=1, source_target_pairs={{0,8},{8,16},{16,24},{24,0},{32,40},{40,48},{48,56},{56,32},{64,72... | collective-permute-start | bytes 1572872 | tf_op jit(solution)/shard_map/ppermute | solution.py:34
  109.3 10.7 %collective-permute-start.22 = (bf16[128,1024]{1,0:T(8,128)(2,1)S(1)}, bf16[128,1024]{1,0:T(8,128)(2,1)S(1)}, u32[]{:S(2)}, u32[]{:S(2)}) collective-permute-start(bf16[128,1024]{1,0:T(8,128)(2,1)S(1)} %get-tuple-element.216), channel_id=1, source_target_pairs={{0,16},{8,24},{16,0},{24,8},{32,48},{40,56},{48,32},{56,40},{64,80... | collective-permute-start | bytes 786440 | tf_op jit(solution)/shard_map/ppermute | solution.py:34
  109.3 15.2 %collective-permute-start.23 = (bf16[128,1024]{1,0:T(8,128)(2,1)S(1)}, bf16[128,1024]{1,0:T(8,128)(2,1)S(1)}, u32[]{:S(2)}, u32[]{:S(2)}) collective-permute-start(bf16[128,1024]{1,0:T(8,128)(2,1)S(1)} %get-tuple-element.217), channel_id=1, source_target_pairs={{0,8},{8,16},{16,24},{24,0},{32,40},{40,48},{48,56},{56,32},{64,72... | collective-permute-start | bytes 786440 | tf_op jit(solution)/shard_map/ppermute | solution.py:34
  110.5 14.0 %collective-permute-start.24 = (bf16[128,1024]{1,0:T(8,128)(2,1)S(1)}, bf16[128,1024]{1,0:T(8,128)(2,1)S(1)}, u32[]{:S(2)}, u32[]{:S(2)}) collective-permute-start(bf16[128,1024]{1,0:T(8,128)(2,1)S(1)} %get-tuple-element.218), channel_id=1, source_target_pairs={{0,24},{8,0},{16,8},{24,16},{32,56},{40,32},{48,40},{56,48},{64,88... | collective-permute-start | bytes 786440 | tf_op jit(solution)/shard_map/ppermute | solution.py:34
  112.6 11.9 %collective-permute-start.25 = (bf16[1024,128]{1,0:T(8,128)(2,1)S(1)}, bf16[1024,128]{1,0:T(8,128)(2,1)S(1)}, u32[]{:S(2)}, u32[]{:S(2)}) collective-permute-start(bf16[1024,128]{1,0:T(8,128)(2,1)S(1)} %get-tuple-element.220), channel_id=1, source_target_pairs={{0,64},{8,72},{16,80},{24,88},{32,96},{40,104},{48,112},{56,120},{... | collective-permute-start | bytes 786440 | tf_op jit(solution)/shard_map/ppermute | solution.py:29
  112.8 12.9 %collective-permute-start.26 = (bf16[1024,128]{1,0:T(8,128)(2,1)S(1)}, bf16[1024,128]{1,0:T(8,128)(2,1)S(1)}, u32[]{:S(2)}, u32[]{:S(2)}) collective-permute-start(bf16[1024,128]{1,0:T(8,128)(2,1)S(1)} %get-tuple-element.221), channel_id=1, source_target_pairs={{0,32},{8,40},{16,48},{24,56},{32,64},{40,72},{48,80},{56,88},{64,... | collective-permute-start | bytes 786440 | tf_op jit(solution)/shard_map/ppermute | solution.py:29
  120.0 8.1 %collective-permute-start.27 = (bf16[1024,128]{1,0:T(8,128)(2,1)S(1)}, bf16[1024,128]{1,0:T(8,128)(2,1)S(1)}, u32[]{:S(2)}, u32[]{:S(2)}) collective-permute-start(bf16[1024,128]{1,0:T(8,128)(2,1)S(1)} %get-tuple-element.222), channel_id=1, source_target_pairs={{0,96},{8,104},{16,112},{24,120},{32,0},{40,8},{48,16},{56,24},{64... | collective-permute-start | bytes 786440 | tf_op jit(solution)/shard_map/ppermute | solution.py:29
  (7 other events, 26.7 us)
